TPU v7x, 32 devices: a whole 2x2x4 slice. The times are simulated.
32 devices in a mesh: dp: 8 (over z, y), mp: 4 (over x, core).
Axes of the slice: x: 2, y: 2, z: 4, core: 2. Of those that a mesh axis runs over, the one named last changes fastest.
Arguments:
- tokens: bfloat16 [8192, 8192], P('dp', 'mp'), may hold values from -6 to 6
- cotangent: bfloat16 [8192, 8192], P('dp', 'mp'), may hold values from -6 to 6
- first_factor: bfloat16 [64, 128, 128], P('mp'), may hold values from -0.5 to 0.5
- second_factor: bfloat16 [64, 128, 128], P('mp'), may hold values from -0.5 to 0.5
Outputs:
- output: bfloat16 [8192, 8192], P('dp', 'mp')
- input_grad: bfloat16 [8192, 8192], P('dp', 'mp')
- first_grad: float32 [64, 128, 128], P('mp')
- second_grad: float32 [64, 128, 128], P('mp')
All inputs are finite; a program needn't handle non-finite values.
Results may differ from a plain program's by a relative error of at most 0.007.
Values may be sent and summed in bfloat16 or wider, within the bound.
No kernel may reach another device: no remote copies, remote signals or barrier semaphores. Data moves between devices by JAX's collectives and lax.ppermute only.
A program may use at most 128 MiB of HBM per device.

v0:
```python
import jax
import jax.numpy as jnp
from jax import lax
from jax.sharding import PartitionSpec as P


def gate_terms(xs, grads, zed):
    xf = xs.astype(jnp.float32)
    gf = grads.astype(jnp.float32)
    zf = zed.astype(jnp.float32)
    sig = jax.nn.sigmoid(xf)
    silu = xf * sig
    output = (zf * silu).astype(jnp.bfloat16)
    grad_z = (gf * silu).astype(jnp.bfloat16)
    gate_grad = (gf * zf * sig * (1.0 + xf * (1.0 - sig))).astype(jnp.bfloat16)
    return (output, grad_z, gate_grad)


def shards(tokens, cotangent, first_factor, second_factor):
    nloc, blk, _ = first_factor.shape
    groups = lax.axis_size("mp")
    nblk = nloc * groups
    ratio = blk // nblk
    rows = tokens.shape[0]
    x_three = tokens.reshape(rows, nloc, blk).transpose(1, 2, 0)
    g_three = cotangent.reshape(rows, nloc, blk).transpose(1, 2, 0)
    x_four = x_three.reshape(nloc, nblk, ratio, rows)
    g_four = g_three.reshape(nloc, nblk, ratio, rows)
    w_first = first_factor.reshape(nloc, blk, nblk, ratio)
    w_second = second_factor.reshape(nloc, ratio, nblk, nblk, ratio)
    hidden = jnp.einsum(
        "ixn,ixjc->ijcn", x_three, w_first, preferred_element_type=jnp.float32
    ).astype(jnp.bfloat16)
    gathered = lax.all_to_all(hidden, "mp", split_axis=1, concat_axis=0, tiled=True)
    result = jnp.einsum(
        "ijcn,jciab->ajbn", gathered, w_second, preferred_element_type=jnp.float32
    ).astype(jnp.bfloat16)
    zed = lax.all_to_all(result, "mp", split_axis=0, concat_axis=1, tiled=True)
    output, grad_z, gate_grad = gate_terms(x_four, g_four, zed)
    grad_mixed = lax.all_to_all(grad_z, "mp", split_axis=1, concat_axis=0, tiled=True)
    second_term = jnp.einsum(
        "ijcn,ajbn->jciab", gathered, grad_mixed, preferred_element_type=jnp.float32
    )
    grad_u = jnp.einsum(
        "ajbn,jciab->ijcn", grad_mixed, w_second, preferred_element_type=jnp.float32
    ).astype(jnp.bfloat16)
    grad_hidden = lax.all_to_all(grad_u, "mp", split_axis=0, concat_axis=1, tiled=True)
    first_term = jnp.einsum(
        "ixn,ijcn->ixjc", x_three, grad_hidden, preferred_element_type=jnp.float32
    )
    input_grad = jnp.einsum(
        "ijcn,ixjc->ixn", grad_hidden, w_first, preferred_element_type=jnp.float32
    )
    input_grad = (input_grad + gate_grad.reshape(nloc, blk, rows).astype(jnp.float32)).astype(
        jnp.bfloat16
    )
    scale = 1.0 / jnp.sqrt(jnp.float32(rows * lax.axis_size("dp")))
    first_local = first_term.reshape(nloc, blk, blk) * scale
    second_local = second_term.reshape(nloc, blk, blk) * scale
    first_grad, second_grad = lax.psum((first_local, second_local), "dp")
    output = output.reshape(nloc * blk, rows).transpose(1, 0)
    input_grad = input_grad.reshape(nloc * blk, rows).transpose(1, 0)
    return (output, input_grad, first_grad, second_grad)


def solution(mesh):
    return jax.shard_map(
        shards,
        mesh=mesh,
        in_specs=(P("dp", "mp"), P("dp", "mp"), P("mp", None, None), P("mp", None, None)),
        out_specs=(P("dp", "mp"), P("dp", "mp"), P("mp", None, None), P("mp", None, None)),
        check_vma=False,
    )
```

profile of v0, /device:TPU:0, one launch (start us, length us, event | category | flops | bytes accessed | tf_op | source)
XLA Modules:
  0.0 417.4 jit_solution(9893737709695610479)
XLA Ops:
  7.2 6.4 %copy.91 = bf16[1024,2048]{0,1:T(8,128)(2,1)} copy(bf16[1024,2048]{1,0:T(8,128)(2,1)} %param.4) | data formatting | bytes 8388608 | tf_op args[0]
  13.6 7.8 %copy.101 = f32[16,128,1024]{2,0,1:T(8,128)} copy(bf16[16,128,1024]{2,1,0:T(8,128)(2,1)} %bitcast.96) | data formatting | bytes 12582912 | tf_op jit(solution)/shard_map/convert_element_type | solution.py:8
  21.4 6.9 %copy.99 = f32[1024,2048]{0,1:T(8,128)} copy(bf16[1024,2048]{1,0:T(8,128)(2,1)} %param.5) | data formatting | bytes 12582912 | tf_op jit(solution)/shard_map/convert_element_type | solution.py:9
  28.3 8.4 %copy.100 = f32[16,128,1024]{2,0,1:T(8,128)S(1)} copy(f32[16,128,1024]{2,1,0:T(8,128)} %bitcast.101) | data formatting | bytes 16777216 | tf_op jit(solution)/shard_map/convert_element_type | solution.py:9
  36.7 13.1 %fusion.5 = bf16[16,64,2,1024]{3,1,2,0:T(8,128)(2,1)S(1)} fusion(f32[16,64,2,1024]{3,0,2,1:T(8,128)S(1)} %bitcast.106, f32[16,64,2,1024]{3,0,2,1:T(8,128)S(1)} %bitcast.105), kind=kLoop, calls=%fused_computation.11 | loop fusion | flops 12582912 | bytes 20971520 | tf_op jit(solution)/shard_map/convert_element_type | solution.py:14
  49.8 6.3 %copy.105 = bf16[16,64,2,1024]{3,2,0,1:T(2,128)(2,1)} copy(bf16[16,64,2,1024]{3,1,2,0:T(8,128)(2,1)S(1)} %fusion.5) | data formatting | bytes 8388608 | tf_op jit(solution)/shard_map/convert_element_type | solution.py:14
  56.1 17.6 %all-to-all-start.2 = ((bf16[16,64,2,1024]{3,2,0,1:T(2,128)(2,1)}), bf16[16,64,2,1024]{3,2,0,1:T(2,128)(2,1)}, u32[]{:S(2)}, u32[]{:S(2)}) async-start(bf16[16,64,2,1024]{3,2,0,1:T(2,128)(2,1)} %copy.105), calls=%async_computation.2 | async-start | bytes 8388608 | tf_op jit(solution)/shard_map/all_to_all | solution.py:40
  77.6 6.4 %copy.93 = bf16[16,64,2,1024]{3,2,0,1:T(2,128)(2,1)} copy(bf16[16,64,2,1024]{3,1,2,0:T(8,128)(2,1)S(1)} %convolution_convert_fusion) | data formatting | bytes 8388608 | tf_op jit(solution)/shard_map/convert_element_type | solution.py:33
  84.0 38.5 %all-to-all-done.2 = bf16[16,64,2,1024]{3,2,0,1:T(2,128)(2,1)} async-done(((bf16[16,64,2,1024]{3,2,0,1:T(2,128)(2,1)}), bf16[16,64,2,1024]{3,2,0,1:T(2,128)(2,1)}, u32[]{:S(2)}, u32[]{:S(2)}) %all-to-all-start.2) | async-done | bytes 4194336 | tf_op jit(solution)/shard_map/all_to_all | solution.py:40
  138.1 6.3 %copy.109 = bf16[64,16,2,1024]{3,2,1,0:T(2,128)(2,1)} copy(bf16[64,16,2,1024]{3,0,2,1:T(8,128)(2,1)S(1)} %fusion.8) | data formatting | bytes 8388608 | tf_op jit(solution)/shard_map/convert_element_type | solution.py:46
  144.5 31.1 %all-to-all-done = bf16[16,64,2,1024]{3,2,0,1:T(2,128)(2,1)} async-done(((bf16[16,64,2,1024]{3,2,0,1:T(2,128)(2,1)}), bf16[16,64,2,1024]{3,2,0,1:T(2,128)(2,1)}, u32[]{:S(2)}, u32[]{:S(2)}) %all-to-all-start) | async-done | bytes 4194336 | tf_op jit(solution)/shard_map/all_to_all | solution.py:34
  175.6 5.2 %all-to-all-start.3 = ((bf16[64,16,2,1024]{3,2,1,0:T(2,128)(2,1)}), bf16[64,16,2,1024]{3,2,1,0:T(2,128)(2,1)}, u32[]{:S(2)}, u32[]{:S(2)}) async-start(bf16[64,16,2,1024]{3,2,1,0:T(2,128)(2,1)} %copy.109), calls=%async_computation.3 | async-start | bytes 8388608 | tf_op jit(solution)/shard_map/all_to_all | solution.py:47
  187.6 6.4 %copy.97 = bf16[64,16,2,1024]{3,2,1,0:T(2,128)(2,1)} copy(bf16[64,16,2,1024]{3,0,2,1:T(8,128)(2,1)S(1)} %fusion.7) | data formatting | bytes 8388608 | tf_op jit(solution)/shard_map/convert_element_type | solution.py:37
  194.0 35.0 %all-to-all-done.3 = bf16[64,16,2,1024]{3,2,1,0:T(2,128)(2,1)} async-done(((bf16[64,16,2,1024]{3,2,1,0:T(2,128)(2,1)}), bf16[64,16,2,1024]{3,2,1,0:T(2,128)(2,1)}, u32[]{:S(2)}, u32[]{:S(2)}) %all-to-all-start.3) | async-done | bytes 4194336 | tf_op jit(solution)/shard_map/all_to_all | solution.py:47
  234.3 5.8 %multiply_bitcast_fusion = f32[16,2,64,64,2]{2,3,1,4,0:T(8,128)S(1)} fusion(bf16[64,16,2,1024,1]{3,0,4,2,1:T(8,128)(2,1)} %bitcast.108, bf16[64,16,2,1024,1]{3,0,2,4,1:T(8,128)(2,1)} %bitcast.112), kind=kOutput, calls=%fused_computation.18 | convolution fusion | flops 537133056 | bytes 9437184 | tf_op jit(solution)/shard_map/ijcn,ajbn->jciab/dot_general | solution.py:41
  251.1 31.0 %all-to-all-done.1 = bf16[64,16,2,1024]{3,2,1,0:T(2,128)(2,1)} async-done(((bf16[64,16,2,1024]{3,2,1,0:T(2,128)(2,1)}), bf16[64,16,2,1024]{3,2,1,0:T(2,128)(2,1)}, u32[]{:S(2)}, u32[]{:S(2)}) %all-to-all-start.1) | async-done | bytes 4194336 | tf_op jit(solution)/shard_map/all_to_all | solution.py:38
  282.1 8.9 %copy_bitcast_fusion = f32[16,4,16,2,1024]{4,3,2,1,0:T(2,128)} fusion(bf16[4,16,16,2,1024]{4,3,2,1,0:T(2,128)(2,1)} %bitcast.51), kind=kLoop, calls=%fused_computation.12 | loop fusion | flops 2097152 | bytes 12582912 | tf_op jit(solution)/shard_map/convert_element_type | solution.py:10
  290.9 11.1 %reshape.60 = f32[16,128,1024]{2,1,0:T(8,128)} reshape(f32[16,4,16,2,1024]{4,3,2,1,0:T(2,128)} %copy_bitcast_fusion) | data formatting | bytes 16777216 | tf_op jit(solution)/shard_map/convert_element_type | solution.py:10
  302.1 13.1 %fusion = bf16[16,128,1024]{2,1,0:T(8,128)(2,1)} fusion(bf16[16,128,1024]{2,1,0:T(8,128)(2,1)} %bitcast.98, f32[16,128,1024]{2,1,0:T(8,128)} %bitcast.102, f32[16,128,1024]{2,1,0:T(8,128)} %reshape.60, bf16[16,64,2,1024]{3,1,2,0:T(8,128)(2,1)} %bitcast.110, bf16[16,128,64,2]{1,0,3,2:T(8,128)(2,1)S(1)} %bitcast.119), kind=kOutput, calls=%fused_computation.1 | convolution fusion | flops 566231040 | bytes 29884416 | tf_op jit(solution)/shard_map/ijcn,ixjc->ixn/dot_general | solution.py:51
  315.1 11.0 %reshape.56 = f32[2048,1024]{1,0:T(8,128)} reshape(f32[16,4,16,2,1024]{4,3,2,1,0:T(2,128)} %copy_bitcast_fusion) | data formatting | bytes 16777216 | tf_op jit(solution)/shard_map/convert_element_type | solution.py:10
  326.1 6.4 %copy.112 = bf16[2048,1024]{0,1:T(8,128)(2,1)} copy(bf16[2048,1024]{1,0:T(8,128)(2,1)} %bitcast.116) | data formatting | bytes 8388608 | tf_op jit(solution)/shard_map/reshape | solution.py:62
  332.5 7.4 %fusion.6 = bf16[2048,1024]{1,0:T(8,128)(2,1)} fusion(f32[2048,1024]{1,0:T(8,128)} %reshape.56, bf16[16,128,1024]{2,1,0:T(8,128)(2,1)} %bitcast.99), kind=kLoop, calls=%fused_computation.14 | loop fusion | flops 14680064 | bytes 16777216 | tf_op jit(solution)/shard_map/convert_element_type | solution.py:13
  340.0 6.4 %copy.115 = bf16[1024,2048]{1,0:T(8,128)(2,1)} copy(bf16[1024,2048]{0,1:T(8,128)(2,1)} %bitcast.114) | data formatting | bytes 8388608
  346.4 58.8 %all-reduce.3.cloned.1.call-done = (f32[16,128,128]{1,0,2:T(8,128)}, f32[16,128,128]{1,2,0:T(8,128)}) async-done(((f32[16,128,128]{1,0,2:T(8,128)}, f32[16,128,128]{1,2,0:T(8,128)}), (f32[16,128,128]{1,0,2:T(8,128)}, f32[16,128,128]{1,2,0:T(8,128)})) %all-reduce.3.cloned.1.call-update) | async-done | bytes 2097168 | tf_op jit(solution)/shard_map/psum | solution.py:60
  (37 shorter events, 47.7 us)
Async XLA Ops:
  28.3 8.4 %slice-start = ((s8[8388608]{0:T(1024)(128)(4,1)}), s8[4194304]{0:T(1024)(128)(4,1)S(1)}, s32[]{:S(2)}) async-start(s8[8388608]{0:T(1024)(128)(4,1)} %bitcast.103), calls=%async_computation.5 | async-start | bytes 8388608
  28.3 8.4 %slice-start.1 = ((s8[8388608]{0:T(1024)(128)(4,1)}), s8[4194304]{0:T(1024)(128)(4,1)S(1)}, s32[]{:S(2)}) async-start(s8[8388608]{0:T(1024)(128)(4,1)} %bitcast.103), calls=%async_computation.6 | async-start | bytes 8388608
  56.1 17.6 %copy-start.4 = (bf16[16,128,128]{2,1,0:T(8,128)(2,1)S(1)}, bf16[16,128,128]{2,1,0:T(8,128)(2,1)}, u32[]{:S(2)}) copy-start(bf16[16,128,128]{2,1,0:T(8,128)(2,1)} %param.6) | copy-start | bytes 1572868
  56.1 66.4 %all-to-all-start.2 = ((bf16[16,64,2,1024]{3,2,0,1:T(2,128)(2,1)}), bf16[16,64,2,1024]{3,2,0,1:T(2,128)(2,1)}, u32[]{:S(2)}, u32[]{:S(2)}) async-start(bf16[16,64,2,1024]{3,2,0,1:T(2,128)(2,1)} %copy.105), calls=%async_computation.2 | async-start | bytes 8388608 | tf_op jit(solution)/shard_map/all_to_all | solution.py:40
  84.0 43.4 %copy-start.5 = (bf16[16,128,128]{2,1,0:T(8,128)(2,1)S(1)}, bf16[16,128,128]{2,1,0:T(8,128)(2,1)}, u32[]{:S(2)}) copy-start(bf16[16,128,128]{2,1,0:T(8,128)(2,1)} %param.7) | copy-start | bytes 1572868
  122.5 53.1 %all-to-all-start = ((bf16[16,64,2,1024]{3,2,0,1:T(2,128)(2,1)}), bf16[16,64,2,1024]{3,2,0,1:T(2,128)(2,1)}, u32[]{:S(2)}, u32[]{:S(2)}) async-start(bf16[16,64,2,1024]{3,2,0,1:T(2,128)(2,1)} %copy.93), calls=%async_computation | async-start | bytes 8388608 | tf_op jit(solution)/shard_map/all_to_all | solution.py:34
  134.9 1.9 copy-start.1
  175.6 53.4 %all-to-all-start.3 = ((bf16[64,16,2,1024]{3,2,1,0:T(2,128)(2,1)}), bf16[64,16,2,1024]{3,2,1,0:T(2,128)(2,1)}, u32[]{:S(2)}, u32[]{:S(2)}) async-start(bf16[64,16,2,1024]{3,2,1,0:T(2,128)(2,1)} %copy.109), calls=%async_computation.3 | async-start | bytes 8388608 | tf_op jit(solution)/shard_map/all_to_all | solution.py:47
  184.3 2.0 copy-start.3
  229.0 53.1 %all-to-all-start.1 = ((bf16[64,16,2,1024]{3,2,1,0:T(2,128)(2,1)}), bf16[64,16,2,1024]{3,2,1,0:T(2,128)(2,1)}, u32[]{:S(2)}, u32[]{:S(2)}) async-start(bf16[64,16,2,1024]{3,2,1,0:T(2,128)(2,1)} %copy.97), calls=%async_computation.1 | async-start | bytes 8388608 | tf_op jit(solution)/shard_map/all_to_all | solution.py:38
  233.8 171.4 %all-reduce.3.cloned.1.call-start = ((), (), s32[]{:S(2)}) async-start(), calls=%async_computation.4 | async-start | bytes 4194304 | tf_op jit(solution)/shard_map/psum | solution.py:60
  243.8 3.7 copy-start
  247.5 2.0 copy-start.2
Sparse Core Ops, SparseCore 0:
  302.2 103.0 all-reduce.2
where the time goes:
time: 425 us; the launch traced here: 417 us
  waiting for transfers between devices  194 us (46%)
  local copies, waits for them, and re-layouts  120 us (28%)
  starting transfers between devices  32.9 us (8%)
  other arithmetic  29.4 us (7%)
  matrix products  26.1 us (6%)
  between operations  14.4 us (3%)
    psum x1, waiting for transfers between devices, shards(): first_grad, second_grad = lax.psum((first_local, second_local), 'dp')  58.8 us
    all_to_all x1, waiting for transfers between devices, shards(): lax.all_to_all(grad_z, 'mp', split_axis=1, concat_axis=0, tiled=True)  38.5 us
    all_to_all x1, waiting for transfers between devices, shards(): lax.all_to_all(grad_u, 'mp', split_axis=0, concat_axis=1, tiled=True)  35 us
    all_to_all x1, waiting for transfers between devices, shards(): lax.all_to_all(hidden, 'mp', split_axis=1, concat_axis=0, tiled=True)  31.1 us
    all_to_all x1, waiting for transfers between devices, shards(): zed = lax.all_to_all(result, 'mp', split_axis=0, concat_axis=1, tiled=True)  31 us
    unnamed x22, local copies, waits for them, and re-layouts  23.2 us
    convert_element_type x2, local copies, waits for them, and re-layouts, gate_terms(): zf = zed.astype(jnp.float32)  22.1 us
    all_to_all x1, starting transfers between devices, shards(): lax.all_to_all(grad_z, 'mp', split_axis=1, concat_axis=0, tiled=True)  17.6 us
  transfers between devices with their start and end apart: 5, of which 5 were waited for; matrix products, arithmetic and copies ran while one was open for 23% of the time, Pallas kernels for 0%

commit v1 on v0

v1 whole, which is shorter than its diff:
```python
import functools

import jax
import jax.numpy as jnp
from jax import lax
from jax.experimental import pallas as pl
from jax.experimental.pallas import tpu as pltpu
from jax.sharding import PartitionSpec as P

BF16, F32 = jnp.bfloat16, jnp.float32
SMEM = pl.BlockSpec(memory_space=pltpu.SMEM)
VMEM_LIMIT = 16 * 2**20
SPAN = 256
GROUP = 256


class Plan:
    def __init__(self, rows, nloc, blk, groups):
        self.rows, self.nloc, self.blk, self.groups = rows, nloc, blk, groups
        self.ratio = blk // (nloc * groups)
        self.piece = self.ratio * nloc
        self.wire = nloc * self.piece
        self.tile = GROUP // nloc
        self.ngroup = nloc * blk // GROUP
        self.span = min(SPAN, rows)


def iotas(size):
    return (
        lax.broadcasted_iota(jnp.int32, (size, size), 0),
        lax.broadcasted_iota(jnp.int32, (size, size), 1),
    )


def onehot(mask):
    return jnp.where(mask, 1.0, 0.0).astype(BF16)


def relative(plan, me):
    r, c = iotas(plan.blk)
    return onehot((r ^ c) == me * plan.piece)


def source_order(plan, me):
    r, c = iotas(plan.blk)
    nblk = plan.nloc * plan.groups
    return onehot(c == (r & (plan.ratio - 1)) * nblk + ((r // plan.ratio) ^ (me * plan.nloc)))


def regroup(plan, back):
    r, c = iotas(GROUP)
    if back:
        r, c = c, r
    return onehot(
        c
        == ((r & (plan.tile - 1)) // plan.ratio) * plan.piece
        + (r // plan.tile) * plan.ratio
        + (r & (plan.ratio - 1))
    )


def dot(a, b, dims):
    return lax.dot_general(a, b, (dims, ((), ())), preferred_element_type=F32)


NN, NT, TN = ((1,), (0,)), ((1,), (1,)), ((0,), (0,))


def join(parts):
    return parts[0] if len(parts) == 1 else jnp.concatenate(parts, axis=0)


def scatter(plan, value, outs, block):
    piece = plan.piece
    at = slice(block * piece, (block + 1) * piece)
    for e in range(plan.groups):
        part = value[e * piece : (e + 1) * piece].astype(BF16)
        outs[e][at, :] = part


def gather(plan, refs, block):
    piece = plan.piece
    parts = []
    for ref in refs:
        part = ref[block * piece : (block + 1) * piece, :]
        parts.append(part if piece % 16 == 0 else part.astype(F32))
    return jnp.concatenate(parts, axis=0).astype(BF16)


def params(count=1):
    return pltpu.CompilerParams(
        dimension_semantics=("arbitrary",) * count, vmem_limit_bytes=VMEM_LIMIT
    )


def cost(flops, moved):
    return pl.CostEstimate(flops=int(flops), bytes_accessed=int(moved), transcendentals=0)


def sends(plan, size, step):
    shapes = [jax.ShapeDtypeStruct((plan.wire, size), BF16)] * plan.groups
    return shapes, arrivals(plan, size, step)


def arrivals(plan, size, step, inside=0):
    at = inside // size
    return [pl.BlockSpec((step * plan.piece, size), lambda i: (i, at))] * plan.groups


def call(kernel, args, in_specs, after=(), into=None, **kwargs):
    count = len(args)
    if into is not None:
        after = [into, *after]
        kwargs["input_output_aliases"] = {count: 0}
    extra = len(after)

    def body(*refs):
        kernel(*refs[:count], *refs[count + extra :])

    return pl.pallas_call(
        body,
        in_specs=list(in_specs) + [pl.BlockSpec(memory_space=pl.ANY)] * extra,
        **kwargs,
    )(*args, *after)


def hold(arrays, after):
    count = len(arrays)
    anywhere = pl.BlockSpec(memory_space=pl.ANY)
    return pl.pallas_call(
        lambda *refs: None,
        out_shape=[pltpu.HBM(a.shape, a.dtype) for a in arrays],
        in_specs=[anywhere] * (count + len(after)),
        out_specs=[anywhere] * count,
        input_output_aliases={i: i for i in range(count)},
        name="hold",
    )(*arrays, *after)


def prepare(plan, me, first, second, after=()):
    def kernel(me_ref, f_ref, s_ref, ft_ref, s_out, st_out):
        rel = relative(plan, me_ref[0])
        order = source_order(plan, me_ref[0])
        for i in range(plan.nloc):
            ft_ref[i] = dot(rel, f_ref[i], NT).astype(BF16)
            rows = dot(order, s_ref[i], NN).astype(BF16)
            s_out[i] = dot(rows, rel, NN).astype(BF16)
            st_out[i] = dot(rel, rows, NT).astype(BF16)

    shape = jax.ShapeDtypeStruct(first.shape, BF16)
    return call(
        kernel,
        (me, first, second),
        [SMEM] + [pl.BlockSpec(memory_space=pltpu.VMEM)] * 2,
        after,
        out_shape=[shape] * 3,
        out_specs=[pl.BlockSpec(memory_space=pltpu.VMEM)] * 3,
        compiler_params=pltpu.CompilerParams(vmem_limit_bytes=VMEM_LIMIT),
        cost_estimate=cost(8 * plan.nloc * plan.blk**3, 5 * first.size * 2),
        name="prepare_factors",
    )


def send_grad_z(plan, me, tokens, cotangent, start, size, after=()):
    step = min(4, plan.nloc)
    shapes, specs = sends(plan, size, step)

    def kernel(me_ref, x_ref, g_ref, *outs):
        rel = relative(plan, me_ref[0])
        for i in range(step):
            cols = slice(i * plan.blk, (i + 1) * plan.blk)
            xf = x_ref[:, cols].astype(F32)
            silu = xf * jax.nn.sigmoid(xf)
            grad_z = (g_ref[:, cols].astype(F32) * silu).astype(BF16)
            scatter(plan, dot(rel, grad_z, NT), outs, i)

    block = pl.BlockSpec((size, step * plan.blk), lambda i: (start // size, i))
    return call(
        kernel,
        (me, tokens, cotangent),
        [SMEM, block, block],
        after,
        grid=(plan.nloc // step,),
        out_shape=shapes,
        out_specs=specs,
        compiler_params=params(),
        cost_estimate=cost(2 * size * plan.nloc * plan.blk**2, 6 * size * plan.nloc * plan.blk),
        name="send_grad_z",
    )


def send_hidden(plan, tokens, first_t, start, size, after=()):
    step = min(4, plan.nloc)
    shapes, specs = sends(plan, size, step)

    def kernel(x_ref, w_ref, *outs):
        for i in range(step):
            cols = slice(i * plan.blk, (i + 1) * plan.blk)
            scatter(plan, dot(w_ref[i], x_ref[:, cols], NT), outs, i)

    return call(
        kernel,
        (tokens, first_t),
        [
            pl.BlockSpec((size, step * plan.blk), lambda i: (start // size, i)),
            pl.BlockSpec((step, plan.blk, plan.blk), lambda i: (i, 0, 0)),
        ],
        after,
        grid=(plan.nloc // step,),
        out_shape=shapes,
        out_specs=specs,
        compiler_params=params(),
        cost_estimate=cost(2 * size * plan.nloc * plan.blk**2, 4 * size * plan.nloc * plan.blk),
        name="send_hidden",
    )


def to_blocks(plan, refs, out):
    matrix = regroup(plan, False)
    for g in range(plan.ngroup):
        begin, parts = g * GROUP, []
        while begin < (g + 1) * GROUP:
            e, inside = begin // plan.wire, begin % plan.wire
            take = min(plan.wire - inside, (g + 1) * GROUP - begin)
            parts.append(refs[e][inside : inside + take, :])
            begin += take
        moved = dot(matrix, join(parts), NN).astype(BF16)
        for j in range(plan.nloc):
            out[j, g * plan.tile : (g + 1) * plan.tile, :] = moved[
                j * plan.tile : (j + 1) * plan.tile
            ]


def from_blocks(plan, held, outs):
    matrix = regroup(plan, True)
    for g in range(plan.ngroup):
        rows = join([held[j, g * plan.tile : (g + 1) * plan.tile, :] for j in range(plan.nloc)])
        moved = dot(matrix, rows, NN).astype(BF16)
        begin = g * GROUP
        while begin < (g + 1) * GROUP:
            e, inside = begin // plan.wire, begin % plan.wire
            take = min(plan.wire - inside, (g + 1) * GROUP - begin)
            part = moved[begin - g * GROUP : begin - g * GROUP + take]
            at = slice(inside, inside + take)
            outs[e][at, :] = part
            begin += take


def whole_spec(shape):
    return pl.BlockSpec(shape, lambda i: (0,) * len(shape))


def own_grad_mixed(plan, arrived, size, after=()):
    count = len(arrived)
    kept = (plan.nloc, plan.blk, size)

    def kernel(*refs):
        to_blocks(plan, refs[:count], refs[count])

    return call(
        kernel,
        list(arrived),
        arrivals(plan, size, plan.nloc),
        after,
        grid=(1,),
        out_shape=pltpu.VMEM(kept, BF16),
        out_specs=whole_spec(kept),
        compiler_params=params(),
        cost_estimate=cost(
            4 * size * plan.nloc * plan.blk**2, 4 * size * plan.nloc * plan.blk
        ),
        name="own_grad_mixed",
    )


def own_u(plan, me, arrived, grad_mixed, total, into, start, size, scale, after=()):
    count = len(arrived)
    kept = (plan.nloc, plan.blk, size)
    square = (plan.nloc, plan.blk, plan.blk)
    extra = [] if total is None else [total]

    def kernel(*refs):
        me_ref, ins, g_ref = refs[0], refs[1 : 1 + count], refs[1 + count]
        u_ref, sum_ref = refs[-2:]
        to_blocks(plan, ins, u_ref)
        if scale is not None:
            rel, order = relative(plan, me_ref[0]), source_order(plan, me_ref[0])
        for j in range(plan.nloc):
            term = dot(u_ref[j], g_ref[j], NT)
            if extra:
                term = term + refs[2 + count][j]
            if scale is not None:
                term = term * scale
                high = term.astype(BF16)
                low = (term - high.astype(F32)).astype(BF16)
                high = dot(dot(order, high, TN).astype(BF16), rel, NN)
                term = high + dot(dot(order, low, TN).astype(BF16), rel, NN)
            sum_ref[j] = term

    return call(
        kernel,
        [me] + list(arrived) + [grad_mixed] + extra,
        [SMEM]
        + arrivals(plan, size, plan.nloc)
        + [whole_spec(kept)]
        + [whole_spec(square)] * len(extra),
        after,
        into,
        grid=(1,),
        out_shape=[
            pltpu.HBM((plan.nloc, plan.blk, plan.rows), BF16),
            jax.ShapeDtypeStruct(square, F32),
        ],
        out_specs=[
            pl.BlockSpec(kept, lambda i: (0, 0, start // size)),
            whole_spec(square),
        ],
        compiler_params=params(),
        cost_estimate=cost(
            6 * size * plan.nloc * plan.blk**2, 6 * size * plan.nloc * plan.blk
        ),
        name="own_u",
    )


def own_product(plan, u, factor, name, start, size, after=()):
    span = plan.span
    shapes, _ = sends(plan, size, plan.nloc)
    shape = (plan.nloc, plan.blk, span)

    def kernel(u_ref, w_ref, *refs):
        outs, held = refs[:-1], refs[-1]
        for j in range(plan.nloc):
            held[j] = dot(w_ref[j], u_ref[j], NN).astype(BF16)
        from_blocks(plan, held, outs)

    return call(
        kernel,
        (u, factor),
        [pl.BlockSpec(shape, lambda t: (0, 0, t + start // span)), whole_spec(factor.shape)],
        after,
        grid=(size // span,),
        out_shape=shapes,
        out_specs=[pl.BlockSpec((plan.wire, span), lambda t: (0, t))] * plan.groups,
        scratch_shapes=[pltpu.VMEM(shape, BF16)],
        compiler_params=params(),
        cost_estimate=cost(
            6 * size * plan.nloc * plan.blk**2, 4 * size * plan.nloc * plan.blk
        ),
        name=name,
    )


def first_term(plan, me, arrived, tokens, total, start, size, scale, after=()):
    count = len(arrived)
    step = min(4, plan.nloc)
    square = pl.BlockSpec((step, plan.blk, plan.blk), lambda i: (i, 0, 0))
    extra = [] if total is None else [total]

    def kernel(*refs):
        me_ref, ins, x_ref, sum_ref = refs[0], refs[1 : 1 + count], refs[1 + count], refs[-1]
        rel = relative(plan, me_ref[0])
        for i in range(step):
            cols = slice(i * plan.blk, (i + 1) * plan.blk)
            term = dot(gather(plan, ins, i), x_ref[:, cols], NN)
            if extra:
                term = term + refs[2 + count][i]
            if scale is not None:
                term = dot((term * scale).astype(BF16), rel, TN)
            sum_ref[i] = term.astype(sum_ref.dtype)

    return call(
        kernel,
        [me] + list(arrived) + [tokens] + extra,
        [SMEM]
        + arrivals(plan, size, step)
        + [pl.BlockSpec((size, step * plan.blk), lambda i: (start // size, i))]
        + [square] * len(extra),
        after,
        grid=(plan.nloc // step,),
        out_shape=jax.ShapeDtypeStruct(
            (plan.nloc, plan.blk, plan.blk), F32 if scale is None else BF16
        ),
        out_specs=square,
        compiler_params=params(),
        cost_estimate=cost(2 * size * plan.nloc * plan.blk**2, 4 * size * plan.nloc * plan.blk),
        name="first_term",
    )


def gate(plan, me, mixed, inside, grads, tokens, cotangent, first_t, held, start, size, after=()):
    count = len(mixed)
    step = min(4, plan.nloc)
    extra = [] if held is None else list(held)

    def kernel(*refs):
        me_ref, zs, hs = refs[0], refs[1 : 1 + count], refs[1 + count : 1 + 2 * count]
        x_ref, g_ref, w_ref = refs[1 + 2 * count : 4 + 2 * count]
        out_ref, grad_ref, done_ref = refs[-3:]
        done_ref[...] = jnp.zeros_like(done_ref)
        rel = relative(plan, me_ref[0])
        for i in range(step):
            cols = slice(i * plan.blk, (i + 1) * plan.blk)
            zf = dot(gather(plan, zs, i), rel, TN)
            back = dot(gather(plan, hs, i), w_ref[i], TN)
            xf = x_ref[:, cols].astype(F32)
            gf = g_ref[:, cols].astype(F32)
            sig = jax.nn.sigmoid(xf)
            out_ref[:, cols] = (zf * (xf * sig)).astype(BF16)
            gate_grad = (gf * zf * sig * (1.0 + xf * (1.0 - sig))).astype(BF16)
            grad_ref[:, cols] = (back + gate_grad.astype(F32)).astype(BF16)

    block = pl.BlockSpec((size, step * plan.blk), lambda i: (start // size, i))
    shape = pltpu.HBM(tokens.shape, BF16)
    before = 4 + 2 * count
    return call(
        kernel,
        [me] + list(mixed) + list(grads) + [tokens, cotangent, first_t] + extra,
        [SMEM]
        + arrivals(plan, size, step, inside)
        + arrivals(plan, size, step)
        + [block, block, pl.BlockSpec((step, plan.blk, plan.blk), lambda i: (i, 0, 0))]
        + [pl.BlockSpec(memory_space=pl.ANY)] * len(extra),
        after,
        grid=(plan.nloc // step,),
        out_shape=[shape, shape, jax.ShapeDtypeStruct((8, 128), F32)],
        out_specs=[block, block, whole_spec((8, 128))],
        input_output_aliases={before: 0, before + 1: 1} if extra else {},
        compiler_params=params(),
        cost_estimate=cost(
            4 * size * plan.nloc * plan.blk**2, 12 * size * plan.nloc * plan.blk
        ),
        name="gate",
    )


def reorder(kernel, args, shapes, name, after=()):
    vmem = pl.BlockSpec(memory_space=pltpu.VMEM)
    moved = sum(a.size for a in args) * 2
    return call(
        kernel,
        args,
        [SMEM] + [vmem] * (len(args) - 1),
        after,
        out_shape=shapes,
        out_specs=[vmem] * len(shapes),
        compiler_params=pltpu.CompilerParams(vmem_limit_bytes=VMEM_LIMIT),
        cost_estimate=cost(moved, 2 * moved),
        name=name,
    )


def halves(place, total, after=()):
    rows, cols = total.shape
    half = rows // 2

    def kernel(place_ref, t_ref, keep_ref, send_ref):
        side = place_ref[0] & 1
        keep_ref[...] = t_ref[pl.ds(pl.multiple_of(side * half, half), half), :]
        send_ref[...] = t_ref[pl.ds(pl.multiple_of((1 - side) * half, half), half), :]

    return reorder(
        kernel, (place, total), [jax.ShapeDtypeStruct((half, cols), BF16)] * 2, "halves", after
    )


def quarters(place, keep, got, count, after=()):
    rows, cols = keep.shape
    part = rows // count

    def kernel(place_ref, a_ref, b_ref, *outs):
        for e in range(count):
            at = pl.multiple_of(((place_ref[0] >> 1) ^ e) * part, part)
            value = a_ref[pl.ds(at, part), :].astype(F32) + b_ref[pl.ds(at, part), :].astype(F32)
            outs[e][...] = value.astype(outs[e].dtype)

    shapes = [jax.ShapeDtypeStruct((part, cols), BF16 if e else F32) for e in range(count)]
    return reorder(kernel, (place, keep, got), shapes, "quarters", after)


def add_up(place, own, others, after=()):
    def kernel(place_ref, own_ref, *refs):
        value = own_ref[...]
        for ref in refs[:-1]:
            value = value + ref[...].astype(F32)
        refs[-1][...] = value.astype(BF16)

    shape = jax.ShapeDtypeStruct(own.shape, BF16)
    return reorder(kernel, (place, own, *others), [shape], "add_up", after)[0]


def join_parts(place, parts, after=()):
    count = len(parts)
    part, cols = parts[0].shape

    def kernel(place_ref, *refs):
        for e in range(count):
            at = pl.multiple_of(((place_ref[0] >> 1) ^ e) * part, part)
            refs[-1][pl.ds(at, part), :] = refs[e][...]

    shape = jax.ShapeDtypeStruct((part * count, cols), BF16)
    return reorder(kernel, (place, *parts), [shape], "join_parts", after)[0]


def join_halves(place, mine, other, after=()):
    half, cols = mine.shape

    def kernel(place_ref, m_ref, o_ref, out_ref):
        side = place_ref[0] & 1
        out_ref[pl.ds(pl.multiple_of(side * half, half), half), :] = m_ref[...].astype(F32)
        out_ref[pl.ds(pl.multiple_of((1 - side) * half, half), half), :] = o_ref[...].astype(F32)

    shape = jax.ShapeDtypeStruct((2 * half, cols), F32)
    return reorder(kernel, (place, mine, other), [shape], "join_halves", after)[0]


def swap(value, by, axis, size):
    return lax.ppermute(value, axis, [(i, i ^ by) for i in range(size)])


def shards(tokens, cotangent, first_factor, second_factor):
    nloc, blk, _ = first_factor.shape
    plan = Plan(tokens.shape[0], nloc, blk, lax.axis_size("mp"))
    rows, parts = plan.rows, lax.axis_size("dp")
    size = plan.span
    chunks = [(start, size) for start in range(0, rows, size)]
    count = len(chunks)
    me = lax.axis_index("mp").astype(jnp.int32).reshape(1)
    scale = float((rows * parts) ** -0.5)
    tokens = pltpu.with_memory_space_constraint(tokens, pltpu.HBM)
    cotangent = pltpu.with_memory_space_constraint(cotangent, pltpu.HBM)
    crossed = []
    order = []

    def after(slot=None):
        found = [] if slot is None or slot < 0 else list(crossed[slot])
        return found + order[-1:]

    def ran(result):
        order.append(result[0] if isinstance(result, (list, tuple)) else result)
        return result

    def send(bufs):
        ran(bufs)
        arrived = [bufs[0]]
        arrived += [swap(v, e, "mp", plan.groups) for e, v in enumerate(bufs[1:], 1)]
        crossed.append(arrived[2:])
        return arrived

    def hbm(arrays):
        return [pltpu.with_memory_space_constraint(a, pltpu.HBM) for a in arrays]

    grad_z, hidden, kept, grad_u, mixed = [], [], [], [], {}
    sums = dict(first=None, second=None, held=None, u=None)
    last = [None] * (count - 1) + [scale]

    def do_grad_z(k, slot):
        grad_z.append(send(send_grad_z(plan, me, tokens, cotangent, *chunks[k], after(slot))))

    def do_hidden(k, slot):
        hidden.append(send(send_hidden(plan, tokens, first_t, *chunks[k], after(slot))))

    def do_kept(k):
        kept.append(ran(own_grad_mixed(plan, grad_z[k], chunks[k][1], after())))

    def do_grad_u(k, slot):
        args = (plan, kept[k], second, "own_grad_u", 0, size, after(slot))
        grad_u.append(send(own_product(*args)))

    def do_u(k):
        args = (hidden[k], kept[k], sums["second"], sums["u"], *chunks[k], last[k], after())
        sums["u"], sums["second"] = own_u(plan, me, *args)
        ran(sums["second"])

    def do_first(k):
        args = (hbm(grad_u[k]), tokens, sums["first"], *chunks[k], last[k])
        sums["first"] = ran(first_term(plan, me, *args, after()))

    def do_mixed(start, length):
        args = (plan, sums["u"], second_t, "own_mixed", start, length, after())
        return ran(own_product(*args))

    def send_mixed(bufs, start, length, slot):
        arrived = send(hold(bufs, after(slot)))
        for k in range(count):
            if start <= chunks[k][0] < start + length:
                mixed[k] = (arrived, chunks[k][0] - start)

    def do_gate(k, slot, extra=()):
        arrived, inside = mixed[k]
        args = (hbm(arrived), inside, hbm(grad_u[k]), tokens, cotangent, first_t, sums["held"])
        *held, done = gate(plan, me, *args, *chunks[k], after(slot) + list(extra))
        sums["held"] = held
        ran(done)

    place = lax.axis_index("dp").astype(jnp.int32).reshape(1)
    state = []

    def split(slot):
        total = sums["first"].reshape(nloc * blk, blk)
        state[:] = ran(halves(place, total, after(slot)))
        state[1] = swap(state[1], 1, "dp", parts)

    def reduce(slot):
        state[:] = ran(quarters(place, *state, parts // 2, after(slot)))
        state[1:] = [swap(v, 2 * e, "dp", parts) for e, v in enumerate(state[1:], 1)]

    def add(slot):
        summed = ran(add_up(place, state[0], state[1:], after(slot)))
        state[:] = [summed] + [swap(summed, 2 * e, "dp", parts) for e in range(1, parts // 2)]

    def join(slot):
        mine = ran(join_parts(place, state, after(slot)))
        state[:] = [mine, swap(mine, 1, "dp", parts)]

    def finish(slot):
        state[:] = [ran(join_halves(place, *state[:2], after(slot) + state[2:]))]

    lead = 3
    for k in range(count):
        do_grad_z(k, k - lead)
        if k == min(lead, count) - 1:
            first_t, second, second_t = ran(
                prepare(plan, me, first_factor, second_factor, after())
            )
    for k in range(count):
        do_hidden(k, count + k - lead)
        do_kept(k)
    do_u(0)
    for k in range(count):
        do_grad_u(k, 2 * count + k - lead)
        if k + 1 < count:
            do_u(k + 1)
    second_grad = lax.psum(sums["second"], "dp")
    late = do_mixed(size, rows - size) if count > 1 else None
    early = do_mixed(0, size)
    for k in range(count - 1):
        do_first(k)
    if count > 1:
        send_mixed(late, size, rows - size, 3 * count - 1)
    do_first(count - 1)
    split(None)
    reduce(None)
    send_mixed(early, 0, size, None)
    add(None)
    for k in range(1, count):
        do_gate(k, None, [second_grad] if k == count - 1 else [])
    join(None)
    do_gate(0, None)
    finish(None)
    first_grad = state[0].reshape(nloc, blk, blk)
    held = sums["held"]
    return (held[0], held[1], first_grad, second_grad)


def solution(mesh):
    return jax.shard_map(
        shards,
        mesh=mesh,
        in_specs=(P("dp", "mp"), P("dp", "mp"), P("mp", None, None), P("mp", None, None)),
        out_specs=(P("dp", "mp"), P("dp", "mp"), P("mp", None, None), P("mp", None, None)),
        check_vma=False,
    )
```

time: 425 us -> 236 us (0.56); the launches traced: 417 us -> 234 us
  waiting for transfers between devices: 194 us -> 67.5 us
  local copies, waits for them, and re-layouts: 120 us -> 16 us
  Pallas kernels: 0 us -> 81.8 us
  other arithmetic: 29.4 us -> 0 us
  matrix products: 26.1 us -> 0 us
  starting transfers between devices: 32.9 us -> 54.5 us
    all_to_all x4 -> x0, waiting for transfers between devices: 136 us -> none  [the longest x1 38.5 us: shards(): lax.all_to_all(grad_z, 'mp', split_axis=1, concat_axis=0, tiled=True)]
    pallas_call x0 -> x38, Pallas kernels: none -> 81.8 us  [the longest x36 81.8 us: call(): pl.pallas_call(body, in_specs=list(in_specs) + [pl.BlockSpec(memory_space...]
    convert_element_type x9 -> x0, local copies, waits for them, and re-layouts: 70.5 us -> none  [the longest x2 22.1 us: gate_terms(): zf = zed.astype(jnp.float32)]
    ppermute x0 -> x50, waiting for transfers between devices: none -> 60.6 us  [swap(): return lax.ppermute(value, axis, [(i, i ^ by) for i in range(size)])]
    ppermute x0 -> x50, starting transfers between devices: none -> 54.5 us  [swap(): return lax.ppermute(value, axis, [(i, i ^ by) for i in range(size)])]
    psum x1, waiting for transfers between devices: 58.8 us -> 6.89 us  [shards(): second_grad = lax.psum(sums['second'], 'dp')]
    all_to_all x4 -> x0, starting transfers between devices: 32.5 us -> none  [the longest x1 17.6 us: shards(): lax.all_to_all(grad_z, 'mp', split_axis=1, concat_axis=0, tiled=True)]
    convert_element_type x3 -> x0, other arithmetic: 29.4 us -> none  [the longest x1 13.1 us: gate_terms(): grad_z = (gf * silu).astype(jnp.bfloat16)]
  transfers between devices with their start and end apart: 5 -> 51, of which waited for: 5 -> 21; matrix products, arithmetic and copies ran while one was open for 23% -> 0% of each run, Pallas kernels for 0% -> 32%
where the time goes in v1:
time: 236 us; the launch traced here: 234 us
  Pallas kernels  81.8 us (35%)
  waiting for transfers between devices  67.5 us (29%)
  starting transfers between devices  54.5 us (23%)
  local copies, waits for them, and re-layouts  16 us (7%)
  between operations  14.6 us (6%)
    pallas_call x36, Pallas kernels, call(): pl.pallas_call(body, in_specs=list(in_specs) + [pl.BlockSpec(memory_space...  81.8 us
    ppermute x50, waiting for transfers between devices, swap(): return lax.ppermute(value, axis, [(i, i ^ by) for i in range(size)])  60.6 us
    ppermute x50, starting transfers between devices, swap(): return lax.ppermute(value, axis, [(i, i ^ by) for i in range(size)])  54.5 us
    unnamed x77, local copies, waits for them, and re-layouts  16 us
    psum x1, waiting for transfers between devices, shards(): second_grad = lax.psum(sums['second'], 'dp')  6.89 us
  transfers between devices with their start and end apart: 51, of which 21 were waited for; matrix products, arithmetic and copies ran while one was open for 0% of the time, Pallas kernels for 32%

profile of v1, /device:TPU:0, one launch (start us, length us, event | category | flops | bytes accessed | tf_op | source)
XLA Modules:
  0.0 234.4 jit_solution(1027764404528349739)
XLA Ops:
  10.2 3.0 %send_grad_z.5 = (bf16[512,256]{1,0:T(8,128)(2,1)S(1)}, bf16[512,256]{1,0:T(8,128)(2,1)S(1)}, bf16[512,256]{1,0:T(8,128)(2,1)S(1)}, bf16[512,256]{1,0:T(8,128)(2,1)S(1)}) custom-call(s32[1]{0:T(128)} %bitcast.refs_0_, bf16[1024,2048]{1,0:T(8,128)(2,1)} %refs_9_.7, bf16[1024,2048]{1,0:T(8,128)(2,1)} %refs_10_.7, ...), custom_call_target="tpu_custom_call" | custom-call | flops 134217728 | bytes 3145728 | tf_op jit(solution)/shard_map/send_grad_z/pallas_call | solution.py:120
  18.1 3.1 %send_grad_z.6 = (bf16[512,256]{1,0:T(8,128)(2,1)S(1)}, bf16[512,256]{1,0:T(8,128)(2,1)S(1)}, bf16[512,256]{1,0:T(8,128)(2,1)S(1)}, bf16[512,256]{1,0:T(8,128)(2,1)S(1)}) custom-call(s32[1]{0:T(128)} %bitcast.refs_0_, bf16[1024,2048]{1,0:T(8,128)(2,1)} %refs_9_.7, bf16[1024,2048]{1,0:T(8,128)(2,1)} %refs_10_.7, ...), custom_call_target="tpu_custom_call" | custom-call | flops 134217728 | bytes 3145728 | tf_op jit(solution)/shard_map/send_grad_z/pallas_call | solution.py:120
  25.5 3.6 %collective-permute-done.2.refs_3_.refs_2_ = bf16[512,256]{1,0:T(8,128)(2,1)S(1)} collective-permute-done((bf16[512,256]{1,0:T(8,128)(2,1)S(1)}, bf16[512,256]{1,0:T(8,128)(2,1)S(1)}, u32[]{:S(2)}, u32[]{:S(2)}) %collective-permute-start.2) | collective-permute-done | bytes 262176 | tf_op jit(solution)/shard_map/ppermute | solution.py:518
  29.0 5.2 %collective-permute-done.3.refs_4_.refs_3_ = bf16[512,256]{1,0:T(8,128)(2,1)S(1)} collective-permute-done((bf16[512,256]{1,0:T(8,128)(2,1)S(1)}, bf16[512,256]{1,0:T(8,128)(2,1)S(1)}, u32[]{:S(2)}, u32[]{:S(2)}) %collective-permute-start.3) | collective-permute-done | bytes 262176 | tf_op jit(solution)/shard_map/ppermute | solution.py:518
  37.7 3.2 %send_grad_z.7 = (bf16[512,256]{1,0:T(8,128)(2,1)S(1)}, bf16[512,256]{1,0:T(8,128)(2,1)S(1)}, bf16[512,256]{1,0:T(8,128)(2,1)S(1)}, bf16[512,256]{1,0:T(8,128)(2,1)S(1)}) custom-call(s32[1]{0:T(128)} %bitcast.refs_0_, bf16[1024,2048]{1,0:T(8,128)(2,1)} %refs_9_.7, bf16[1024,2048]{1,0:T(8,128)(2,1)} %refs_10_.7, ...), custom_call_target="tpu_custom_call" | custom-call | flops 134217728 | bytes 3145728 | tf_op jit(solution)/shard_map/send_grad_z/pallas_call | solution.py:120
  46.0 5.1 %collective-permute-done.8.refs_3_ = bf16[512,256]{1,0:T(8,128)(2,1)S(1)} collective-permute-done((bf16[512,256]{1,0:T(8,128)(2,1)S(1)}, bf16[512,256]{1,0:T(8,128)(2,1)S(1)}, u32[]{:S(2)}, u32[]{:S(2)}) %collective-permute-start.8) | collective-permute-done | bytes 262176 | tf_op jit(solution)/shard_map/ppermute | solution.py:518
  53.2 3.9 %collective-permute-done.4.refs_2_.refs_3_ = bf16[512,256]{1,0:T(8,128)(2,1)S(1)} collective-permute-done((bf16[512,256]{1,0:T(8,128)(2,1)S(1)}, bf16[512,256]{1,0:T(8,128)(2,1)S(1)}, u32[]{:S(2)}, u32[]{:S(2)}) %collective-permute-start.4) | collective-permute-done | bytes 262176 | tf_op jit(solution)/shard_map/ppermute | solution.py:518
  62.5 5.8 %collective-permute-done.9.refs_2_ = bf16[512,256]{1,0:T(8,128)(2,1)S(1)} collective-permute-done((bf16[512,256]{1,0:T(8,128)(2,1)S(1)}, bf16[512,256]{1,0:T(8,128)(2,1)S(1)}, u32[]{:S(2)}, u32[]{:S(2)}) %collective-permute-start.9) | collective-permute-done | bytes 262176 | tf_op jit(solution)/shard_map/ppermute | solution.py:518
  70.4 3.1 %collective-permute-done.10.refs_3_ = bf16[512,256]{1,0:T(8,128)(2,1)S(1)} collective-permute-done((bf16[512,256]{1,0:T(8,128)(2,1)S(1)}, bf16[512,256]{1,0:T(8,128)(2,1)S(1)}, u32[]{:S(2)}, u32[]{:S(2)}) %collective-permute-start.10) | collective-permute-done | bytes 262176 | tf_op jit(solution)/shard_map/ppermute | solution.py:518
  90.8 5.2 %collective-permute-done.19.refs_3_.refs_4_ = bf16[512,256]{1,0:T(8,128)(2,1)S(1)} collective-permute-done((bf16[512,256]{1,0:T(8,128)(2,1)S(1)}, bf16[512,256]{1,0:T(8,128)(2,1)S(1)}, u32[]{:S(2)}, u32[]{:S(2)}) %collective-permute-start.19) | collective-permute-done | bytes 262176 | tf_op jit(solution)/shard_map/ppermute | solution.py:518
  102.1 5.2 %collective-permute-done.15.refs_3_.refs_4_ = bf16[512,256]{1,0:T(8,128)(2,1)S(1)} collective-permute-done((bf16[512,256]{1,0:T(8,128)(2,1)S(1)}, bf16[512,256]{1,0:T(8,128)(2,1)S(1)}, u32[]{:S(2)}, u32[]{:S(2)}) %collective-permute-start.15) | collective-permute-done | bytes 262176 | tf_op jit(solution)/shard_map/ppermute | solution.py:518
  109.6 3.7 %collective-permute-done.24.refs_2_.refs_3_.refs_7_ = bf16[512,256]{1,0:T(8,128)(2,1)S(1)} collective-permute-done((bf16[512,256]{1,0:T(8,128)(2,1)S(1)}, bf16[512,256]{1,0:T(8,128)(2,1)S(1)}, u32[]{:S(2)}, u32[]{:S(2)}) %collective-permute-start.24) | collective-permute-done | bytes 262176 | tf_op jit(solution)/shard_map/ppermute | solution.py:518
  116.3 4.9 %own_u.7 = (bf16[16,128,1024]{2,1,0:T(8,128)(2,1)}, f32[16,128,128]{2,1,0:T(8,128)}) custom-call(s32[1]{0:T(128)} %bitcast.refs_0_, bf16[512,256]{1,0:T(8,128)(2,1)S(1)} %get-tuple-element.118.refs_4_.refs_1_, bf16[512,256]{1,0:T(8,128)(2,1)S(1)} %collective-permute-done.13.refs_2_, ...), custom_call_target="tpu_custom_call", output_to_operand_aliasing={{0}: (7, {})} | custom-call | flops 402653184 | bytes 3145728 | tf_op jit(solution)/shard_map/own_u/pallas_call | solution.py:120
  135.0 3.1 %own_mixed.2 = (bf16[512,768]{1,0:T(8,128)(2,1)S(1)}, bf16[512,768]{1,0:T(8,128)(2,1)S(1)}, bf16[512,768]{1,0:T(8,128)(2,1)S(1)}, bf16[512,768]{1,0:T(8,128)(2,1)S(1)}) custom-call(bf16[16,128,1024]{2,1,0:T(8,128)(2,1)S(1)} %copy-done, bf16[16,128,128]{2,1,0:T(8,128)(2,1)S(1)} %copy-done.16, bf16[512,256]{1,0:T(8,128)(2,1)S(1)} %get-tuple-element.145.refs_2_.refs_1_.refs_5_), custom_call_target="tpu_custom_call" | custom-call | flops 1207959552 | bytes 6291456 | tf_op jit(solution)/shard_map/own_mixed/pallas_call | solution.py:120
  140.7 3.2 %first_term.4.refs_6_.refs_7_ = f32[16,128,128]{2,1,0:T(8,128)S(1)} custom-call(s32[1]{0:T(128)} %bitcast.refs_0_, bf16[512,256]{1,0:T(8,128)(2,1)} %copy-done.11, bf16[512,256]{1,0:T(8,128)(2,1)} %copy-done.33, bf16[512,256]{1,0:T(8,128)(2,1)} %copy-done.12, bf16[512,256]{1,0:T(8,128)(2,1)} %copy-done.13, bf16[1024,2048]{1,0:T(8,128)(2,1)} %refs_9_.7, ...), custom_call_target="tpu_custom_call" | custom-call | flops 134217728 | bytes 2097152 | tf_op jit(solution)/shard_map/first_term/pallas_call | solution.py:120
  156.6 5.2 %first_term.7.refs_2_ = bf16[16,128,128]{2,1,0:T(8,128)(2,1)S(1)} custom-call(s32[1]{0:T(128)} %bitcast.refs_0_, bf16[512,256]{1,0:T(8,128)(2,1)} %copy-done.10, bf16[512,256]{1,0:T(8,128)(2,1)} %collective-permute-done.26.refs_2_.refs_6_, bf16[512,256]{1,0:T(8,128)(2,1)} %copy-done.32, bf16[512,256]{1,0:T(8,128)(2,1)} %collective-permute-done.28.refs_5_.refs_4_.refs_8_, ...), custom_call_target="tpu_custom_call" | custom-call | flops 134217728 | bytes 2097152 | tf_op jit(solution)/shard_map/first_term/pallas_call | solution.py:120
  163.7 6.8 %collective-permute-done.36.refs_2_ = bf16[1024,128]{1,0:T(8,128)(2,1)S(1)} collective-permute-done((bf16[1024,128]{1,0:T(8,128)(2,1)S(1)}, bf16[1024,128]{1,0:T(8,128)(2,1)S(1)}, u32[]{:S(2)}, u32[]{:S(2)}) %collective-permute-start.36) | collective-permute-done | bytes 262176 | tf_op jit(solution)/shard_map/ppermute | solution.py:518
  175.6 4.1 %collective-permute-start.45 = (bf16[256,128]{1,0:T(8,128)(2,1)S(1)}, bf16[256,128]{1,0:T(8,128)(2,1)S(1)}, u32[]{:S(2)}, u32[]{:S(2)}) collective-permute-start(bf16[256,128]{1,0:T(8,128)(2,1)S(1)} %get-tuple-element.177), channel_id=1, source_target_pairs={{0,24},{4,28},{8,16},{12,20},{16,8},{20,12},{24,0},{28,4},{1,25},{... | collective-permute-start | bytes 196616 | tf_op jit(solution)/shard_map/ppermute | solution.py:518
  185.9 4.2 %collective-permute-start.47 = (bf16[256,128]{1,0:T(8,128)(2,1)S(1)}, bf16[256,128]{1,0:T(8,128)(2,1)S(1)}, u32[]{:S(2)}, u32[]{:S(2)}) collective-permute-start(bf16[256,128]{1,0:T(8,128)(2,1)S(1)} %add_up.1.refs_12_.refs_1_), channel_id=1, source_target_pairs={{0,16},{4,20},{8,24},{12,28},{16,0},{20,4},{24,8},{28,12},{1,17},{... | collective-permute-start | bytes 196616 | tf_op jit(solution)/shard_map/ppermute | solution.py:518
  192.4 5.2 %gate.4 = (bf16[1024,2048]{1,0:T(8,128)(2,1)}, bf16[1024,2048]{1,0:T(8,128)(2,1)}, f32[8,128]{1,0:T(8,128)S(1)}) custom-call(s32[1]{0:T(128)} %bitcast.refs_0_, bf16[512,768]{1,0:T(8,128)(2,1)} %get-tuple-element.164.refs_7_.refs_1_, bf16[512,768]{1,0:T(8,128)(2,1)} %copy-done.30, bf16[512,768]{1,0:T(8,128)(2,1)} %copy-done.31, ...), custom_call_target="tpu_custom_call" | custom-call | flops 268435456 | bytes 6291456 | tf_op jit(solution)/shard_map/gate/pallas_call | solution.py:120
  197.6 5.2 %gate.5 = (bf16[1024,2048]{1,0:T(8,128)(2,1)}, bf16[1024,2048]{1,0:T(8,128)(2,1)}, f32[8,128]{1,0:T(8,128)S(1)}) custom-call(s32[1]{0:T(128)} %bitcast.refs_0_, bf16[512,768]{1,0:T(8,128)(2,1)} %get-tuple-element.164.refs_7_.refs_1_, bf16[512,768]{1,0:T(8,128)(2,1)} %copy-done.30, ...), custom_call_target="tpu_custom_call", output_to_operand_aliasing={{0}: (12, {}), {1}: (13, {})} | custom-call | flops 268435456 | bytes 6291456 | tf_op jit(solution)/shard_map/gate/pallas_call | solution.py:120
  204.8 6.9 %all-reduce.2.cloned.1.call-done.refs_15_ = f32[16,128,128]{2,1,0:T(8,128)} async-done(((f32[16,128,128]{2,1,0:T(8,128)}), f32[16,128,128]{2,1,0:T(8,128)}) %all-reduce.2.cloned.1.call-update) | async-done | bytes 1048592 | tf_op jit(solution)/shard_map/psum | solution.py:634
  212.9 5.2 %gate.6 = (bf16[1024,2048]{1,0:T(8,128)(2,1)}, bf16[1024,2048]{1,0:T(8,128)(2,1)}, f32[8,128]{1,0:T(8,128)S(1)}) custom-call(s32[1]{0:T(128)} %bitcast.refs_0_, bf16[512,768]{1,0:T(8,128)(2,1)} %get-tuple-element.164.refs_7_.refs_1_, bf16[512,768]{1,0:T(8,128)(2,1)} %copy-done.30, ...), custom_call_target="tpu_custom_call", output_to_operand_aliasing={{0}: (12, {}), {1}: (13, {})} | custom-call | flops 268435456 | bytes 6291456 | tf_op jit(solution)/shard_map/gate/pallas_call | solution.py:120
  220.3 5.2 %gate.7 = (bf16[1024,2048]{1,0:T(8,128)(2,1)}, bf16[1024,2048]{1,0:T(8,128)(2,1)}, f32[8,128]{1,0:T(8,128)S(1)}) custom-call(s32[1]{0:T(128)} %bitcast.refs_0_, bf16[512,256]{1,0:T(8,128)(2,1)} %get-tuple-element.168.refs_5_.refs_1_, bf16[512,256]{1,0:T(8,128)(2,1)} %copy-done.35, ...), custom_call_target="tpu_custom_call", output_to_operand_aliasing={{0}: (12, {}), {1}: (13, {})} | custom-call | flops 268435456 | bytes 6291456 | tf_op jit(solution)/shard_map/gate/pallas_call | solution.py:120
  (194 shorter events, 110.6 us)
Async XLA Ops:
  17.2 23.8 %collective-permute-start.1 = (bf16[512,256]{1,0:T(8,128)(2,1)S(1)}, bf16[512,256]{1,0:T(8,128)(2,1)S(1)}, u32[]{:S(2)}, u32[]{:S(2)}) collective-permute-start(bf16[512,256]{1,0:T(8,128)(2,1)S(1)} %get-tuple-element.102), channel_id=1, source_target_pairs={{0,3},{1,2},{2,1},{3,0},{4,7},{5,6},{6,5},{7,4},{8,11},{9,10},{10,... | collective-permute-start | bytes 786440 | tf_op jit(solution)/shard_map/ppermute | solution.py:518
  21.2 22.4 %collective-permute-start.6 = (bf16[512,256]{1,0:T(8,128)(2,1)S(1)}, bf16[512,256]{1,0:T(8,128)(2,1)S(1)}, u32[]{:S(2)}, u32[]{:S(2)}) collective-permute-start(bf16[512,256]{1,0:T(8,128)(2,1)S(1)} %get-tuple-element.108), channel_id=1, source_target_pairs={{0,1},{1,0},{2,3},{3,2},{4,5},{5,4},{6,7},{7,6},{8,9},{9,8},{10,11... | collective-permute-start | bytes 786440 | tf_op jit(solution)/shard_map/ppermute | solution.py:518
  23.4 22.5 %collective-permute-start.7 = (bf16[512,256]{1,0:T(8,128)(2,1)S(1)}, bf16[512,256]{1,0:T(8,128)(2,1)S(1)}, u32[]{:S(2)}, u32[]{:S(2)}) collective-permute-start(bf16[512,256]{1,0:T(8,128)(2,1)S(1)} %get-tuple-element.109), channel_id=1, source_target_pairs={{0,2},{1,3},{2,0},{3,1},{4,6},{5,7},{6,4},{7,5},{8,10},{9,11},{10,... | collective-permute-start | bytes 786440 | tf_op jit(solution)/shard_map/ppermute | solution.py:518
  29.0 22.0 %collective-permute-start.8 = (bf16[512,256]{1,0:T(8,128)(2,1)S(1)}, bf16[512,256]{1,0:T(8,128)(2,1)S(1)}, u32[]{:S(2)}, u32[]{:S(2)}) collective-permute-start(bf16[512,256]{1,0:T(8,128)(2,1)S(1)} %get-tuple-element.110), channel_id=1, source_target_pairs={{0,3},{1,2},{2,1},{3,0},{4,7},{5,6},{6,5},{7,4},{8,11},{9,10},{10,... | collective-permute-start | bytes 786440 | tf_op jit(solution)/shard_map/ppermute | solution.py:518
  51.3 22.3 %collective-permute-start.10 = (bf16[512,256]{1,0:T(8,128)(2,1)S(1)}, bf16[512,256]{1,0:T(8,128)(2,1)S(1)}, u32[]{:S(2)}, u32[]{:S(2)}) collective-permute-start(bf16[512,256]{1,0:T(8,128)(2,1)S(1)} %get-tuple-element.112), channel_id=1, source_target_pairs={{0,3},{1,2},{2,1},{3,0},{4,7},{5,6},{6,5},{7,4},{8,11},{9,10},{10,... | collective-permute-start | bytes 786440 | tf_op jit(solution)/shard_map/ppermute | solution.py:518
  53.0 25.5 %collective-permute-start.16 = (bf16[512,256]{1,0:T(8,128)(2,1)S(1)}, bf16[512,256]{1,0:T(8,128)(2,1)S(1)}, u32[]{:S(2)}, u32[]{:S(2)}) collective-permute-start(bf16[512,256]{1,0:T(8,128)(2,1)S(1)} %get-tuple-element.122), channel_id=1, source_target_pairs={{0,1},{1,0},{2,3},{3,2},{4,5},{5,4},{6,7},{7,6},{8,9},{9,8},{10,11... | collective-permute-start | bytes 786440 | tf_op jit(solution)/shard_map/ppermute | solution.py:518
  57.1 21.5 %collective-permute-start.23 = (bf16[512,256]{1,0:T(8,128)(2,1)S(1)}, bf16[512,256]{1,0:T(8,128)(2,1)S(1)}, u32[]{:S(2)}, u32[]{:S(2)}) collective-permute-start(bf16[512,256]{1,0:T(8,128)(2,1)S(1)} %get-tuple-element.129), channel_id=1, source_target_pairs={{0,1},{1,0},{2,3},{3,2},{4,5},{5,4},{6,7},{7,6},{8,9},{9,8},{10,11... | collective-permute-start | bytes 786440 | tf_op jit(solution)/shard_map/ppermute | solution.py:518
  62.3 21.6 %collective-permute-start.20 = (bf16[512,256]{1,0:T(8,128)(2,1)S(1)}, bf16[512,256]{1,0:T(8,128)(2,1)S(1)}, u32[]{:S(2)}, u32[]{:S(2)}) collective-permute-start(bf16[512,256]{1,0:T(8,128)(2,1)S(1)} %get-tuple-element.126), channel_id=1, source_target_pairs={{0,1},{1,0},{2,3},{3,2},{4,5},{5,4},{6,7},{7,6},{8,9},{9,8},{10,11... | collective-permute-start | bytes 786440 | tf_op jit(solution)/shard_map/ppermute | solution.py:518
  86.0 21.2 %collective-permute-start.15 = (bf16[512,256]{1,0:T(8,128)(2,1)S(1)}, bf16[512,256]{1,0:T(8,128)(2,1)S(1)}, u32[]{:S(2)}, u32[]{:S(2)}) collective-permute-start(bf16[512,256]{1,0:T(8,128)(2,1)S(1)} %get-tuple-element.121), channel_id=1, source_target_pairs={{0,3},{1,2},{2,1},{3,0},{4,7},{5,6},{6,5},{7,4},{8,11},{9,10},{10,... | collective-permute-start | bytes 786440 | tf_op jit(solution)/shard_map/ppermute | solution.py:518
  99.2 22.0 %collective-permute-start.25 = (bf16[512,256]{1,0:T(8,128)(2,1)S(1)}, bf16[512,256]{1,0:T(8,128)(2,1)S(1)}, u32[]{:S(2)}, u32[]{:S(2)}) collective-permute-start(bf16[512,256]{1,0:T(8,128)(2,1)S(1)} %get-tuple-element.143), channel_id=1, source_target_pairs={{0,3},{1,2},{2,1},{3,0},{4,7},{5,6},{6,5},{7,4},{8,11},{9,10},{10,... | collective-permute-start | bytes 786440 | tf_op jit(solution)/shard_map/ppermute | solution.py:518
  102.1 21.3 %collective-permute-start.35 = (bf16[512,256]{1,0:T(8,128)(2,1)S(1)}, bf16[512,256]{1,0:T(8,128)(2,1)S(1)}, u32[]{:S(2)}, u32[]{:S(2)}) collective-permute-start(bf16[512,256]{1,0:T(8,128)(2,1)S(1)} %get-tuple-element.160), channel_id=1, source_target_pairs={{0,1},{1,0},{2,3},{3,2},{4,5},{5,4},{6,7},{7,6},{8,9},{9,8},{10,11... | collective-permute-start | bytes 786440 | tf_op jit(solution)/shard_map/ppermute | solution.py:518
  121.2 25.8 %collective-permute-start.29 = (bf16[512,256]{1,0:T(8,128)(2,1)}, bf16[512,256]{1,0:T(8,128)(2,1)}, u32[]{:S(2)}, u32[]{:S(2)}) collective-permute-start(bf16[512,256]{1,0:T(8,128)(2,1)} %get-tuple-element.154), channel_id=1, source_target_pairs={{0,1},{1,0},{2,3},{3,2},{4,5},{5,4},{6,7},{7,6},{8,9},{9,8},{10,11... | collective-permute-start | bytes 786440 | tf_op jit(solution)/shard_map/ppermute | solution.py:518
  123.4 23.6 %collective-permute-start.30 = (bf16[512,256]{1,0:T(8,128)(2,1)}, bf16[512,256]{1,0:T(8,128)(2,1)}, u32[]{:S(2)}, u32[]{:S(2)}) collective-permute-start(bf16[512,256]{1,0:T(8,128)(2,1)} %get-tuple-element.155), channel_id=1, source_target_pairs={{0,2},{1,3},{2,0},{3,1},{4,6},{5,7},{6,4},{7,5},{8,10},{9,11},{10,... | collective-permute-start | bytes 786440 | tf_op jit(solution)/shard_map/ppermute | solution.py:518
  124.8 22.2 %collective-permute-start.31 = (bf16[512,256]{1,0:T(8,128)(2,1)}, bf16[512,256]{1,0:T(8,128)(2,1)}, u32[]{:S(2)}, u32[]{:S(2)}) collective-permute-start(bf16[512,256]{1,0:T(8,128)(2,1)} %get-tuple-element.156), channel_id=1, source_target_pairs={{0,3},{1,2},{2,1},{3,0},{4,7},{5,6},{6,5},{7,4},{8,11},{9,10},{10,... | collective-permute-start | bytes 786440 | tf_op jit(solution)/shard_map/ppermute | solution.py:518
  127.7 83.9 %all-reduce.2.cloned.1.call-start = ((), (), s32[]{:S(2)}) async-start(), calls=%async_computation | async-start | bytes 2097152 | tf_op jit(solution)/shard_map/psum | solution.py:634
  127.7 23.1 %collective-permute-start.27 = (bf16[512,256]{1,0:T(8,128)(2,1)}, bf16[512,256]{1,0:T(8,128)(2,1)S(1)}, u32[]{:S(2)}, u32[]{:S(2)}) collective-permute-start(bf16[512,256]{1,0:T(8,128)(2,1)} %copy-done.29), channel_id=1, source_target_pairs={{0,2},{1,3},{2,0},{3,1},{4,6},{5,7},{6,4},{7,5},{8,10},{9,11},{10,... | collective-permute-start | bytes 786440 | tf_op jit(solution)/shard_map/ppermute | solution.py:518
  129.8 21.3 %collective-permute-start.28 = (bf16[512,256]{1,0:T(8,128)(2,1)}, bf16[512,256]{1,0:T(8,128)(2,1)}, u32[]{:S(2)}, u32[]{:S(2)}) collective-permute-start(bf16[512,256]{1,0:T(8,128)(2,1)} %copy-done.28), channel_id=1, source_target_pairs={{0,3},{1,2},{2,1},{3,0},{4,7},{5,6},{6,5},{7,4},{8,11},{9,10},{10,... | collective-permute-start | bytes 786440 | tf_op jit(solution)/shard_map/ppermute | solution.py:518
  151.6 32.8 %collective-permute-start.40 = (bf16[512,768]{1,0:T(8,128)(2,1)}, bf16[512,768]{1,0:T(8,128)(2,1)S(1)}, u32[]{:S(2)}, u32[]{:S(2)}) collective-permute-start(bf16[512,768]{1,0:T(8,128)(2,1)} %get-tuple-element.172), channel_id=1, source_target_pairs={{0,1},{1,0},{2,3},{3,2},{4,5},{5,4},{6,7},{7,6},{8,9},{9,8},{10,11... | collective-permute-start | bytes 2359304 | tf_op jit(solution)/shard_map/ppermute | solution.py:518
  152.0 33.9 %collective-permute-start.41 = (bf16[512,768]{1,0:T(8,128)(2,1)}, bf16[512,768]{1,0:T(8,128)(2,1)S(1)}, u32[]{:S(2)}, u32[]{:S(2)}) collective-permute-start(bf16[512,768]{1,0:T(8,128)(2,1)} %get-tuple-element.173), channel_id=1, source_target_pairs={{0,2},{1,3},{2,0},{3,1},{4,6},{5,7},{6,4},{7,5},{8,10},{9,11},{10,... | collective-permute-start | bytes 2359304 | tf_op jit(solution)/shard_map/ppermute | solution.py:518
  153.7 36.3 %collective-permute-start.42 = (bf16[512,768]{1,0:T(8,128)(2,1)}, bf16[512,768]{1,0:T(8,128)(2,1)}, u32[]{:S(2)}, u32[]{:S(2)}) collective-permute-start(bf16[512,768]{1,0:T(8,128)(2,1)} %get-tuple-element.174), channel_id=1, source_target_pairs={{0,3},{1,2},{2,1},{3,0},{4,7},{5,6},{6,5},{7,4},{8,11},{9,10},{10,... | collective-permute-start | bytes 2359304 | tf_op jit(solution)/shard_map/ppermute | solution.py:518
  184.3 35.2 %collective-permute-start.37 = (bf16[512,256]{1,0:T(8,128)(2,1)}, bf16[512,256]{1,0:T(8,128)(2,1)S(1)}, u32[]{:S(2)}, u32[]{:S(2)}) collective-permute-start(bf16[512,256]{1,0:T(8,128)(2,1)} %get-tuple-element.169), channel_id=1, source_target_pairs={{0,1},{1,0},{2,3},{3,2},{4,5},{5,4},{6,7},{7,6},{8,9},{9,8},{10,11... | collective-permute-start | bytes 786440 | tf_op jit(solution)/shard_map/ppermute | solution.py:518
  184.4 35.1 %collective-permute-start.38 = (bf16[512,256]{1,0:T(8,128)(2,1)}, bf16[512,256]{1,0:T(8,128)(2,1)S(1)}, u32[]{:S(2)}, u32[]{:S(2)}) collective-permute-start(bf16[512,256]{1,0:T(8,128)(2,1)} %get-tuple-element.170), channel_id=1, source_target_pairs={{0,2},{1,3},{2,0},{3,1},{4,6},{5,7},{6,4},{7,5},{8,10},{9,11},{10,... | collective-permute-start | bytes 786440 | tf_op jit(solution)/shard_map/ppermute | solution.py:518
  185.9 32.2 %collective-permute-start.47 = (bf16[256,128]{1,0:T(8,128)(2,1)S(1)}, bf16[256,128]{1,0:T(8,128)(2,1)S(1)}, u32[]{:S(2)}, u32[]{:S(2)}) collective-permute-start(bf16[256,128]{1,0:T(8,128)(2,1)S(1)} %add_up.1.refs_12_.refs_1_), channel_id=1, source_target_pairs={{0,16},{4,20},{8,24},{12,28},{16,0},{20,4},{24,8},{28,12},{1,17},{... | collective-permute-start | bytes 196616 | tf_op jit(solution)/shard_map/ppermute | solution.py:518
  190.1 28.0 %collective-permute-start.48 = (bf16[256,128]{1,0:T(8,128)(2,1)S(1)}, bf16[256,128]{1,0:T(8,128)(2,1)S(1)}, u32[]{:S(2)}, u32[]{:S(2)}) collective-permute-start(bf16[256,128]{1,0:T(8,128)(2,1)S(1)} %add_up.1.refs_12_.refs_1_), channel_id=1, source_target_pairs={{0,24},{4,28},{8,16},{12,20},{16,8},{20,12},{24,0},{28,4},{1,25},{... | collective-permute-start | bytes 196616 | tf_op jit(solution)/shard_map/ppermute | solution.py:518
  (65 other events, 563.2 us)
Sparse Core Ops, SparseCore 0:
  132.6 78.9 all-reduce.1

commit v2 on v1

--- a/solution.py
+++ b/solution.py
@@ -64,6 +64,14 @@
 
 
 NN, NT, TN = ((1,), (0,)), ((1,), (1,)), ((0,), (0,))
+
+
+def sigmoid(x):
+    return 0.5 * jnp.tanh(0.5 * x) + 0.5
+
+
+def in_hbm(array):
+    return pltpu.with_memory_space_constraint(array, pltpu.HBM)
 
 
 def join(parts):
@@ -162,7 +170,7 @@
 
 
 def send_grad_z(plan, me, tokens, cotangent, start, size, after=()):
-    step = min(4, plan.nloc)
+    step = min(8, plan.nloc)
     shapes, specs = sends(plan, size, step)
 
     def kernel(me_ref, x_ref, g_ref, *outs):
@@ -170,7 +178,7 @@
         for i in range(step):
             cols = slice(i * plan.blk, (i + 1) * plan.blk)
             xf = x_ref[:, cols].astype(F32)
-            silu = xf * jax.nn.sigmoid(xf)
+            silu = xf * sigmoid(xf)
             grad_z = (g_ref[:, cols].astype(F32) * silu).astype(BF16)
             scatter(plan, dot(rel, grad_z, NT), outs, i)
 
@@ -190,7 +198,7 @@
 
 
 def send_hidden(plan, tokens, first_t, start, size, after=()):
-    step = min(4, plan.nloc)
+    step = min(8, plan.nloc)
     shapes, specs = sends(plan, size, step)
 
     def kernel(x_ref, w_ref, *outs):
@@ -336,7 +344,7 @@
 
     return call(
         kernel,
-        (u, factor),
+        (u, in_hbm(factor)),
         [pl.BlockSpec(shape, lambda t: (0, 0, t + start // span)), whole_spec(factor.shape)],
         after,
         grid=(size // span,),
@@ -353,7 +361,7 @@
 
 def first_term(plan, me, arrived, tokens, total, start, size, scale, after=()):
     count = len(arrived)
-    step = min(4, plan.nloc)
+    step = min(8, plan.nloc)
     square = pl.BlockSpec((step, plan.blk, plan.blk), lambda i: (i, 0, 0))
     extra = [] if total is None else [total]
 
@@ -390,7 +398,7 @@
 
 def gate(plan, me, mixed, inside, grads, tokens, cotangent, first_t, held, start, size, after=()):
     count = len(mixed)
-    step = min(4, plan.nloc)
+    step = min(8, plan.nloc)
     extra = [] if held is None else list(held)
 
     def kernel(*refs):
@@ -405,9 +413,10 @@
             back = dot(gather(plan, hs, i), w_ref[i], TN)
             xf = x_ref[:, cols].astype(F32)
             gf = g_ref[:, cols].astype(F32)
-            sig = jax.nn.sigmoid(xf)
-            out_ref[:, cols] = (zf * (xf * sig)).astype(BF16)
-            gate_grad = (gf * zf * sig * (1.0 + xf * (1.0 - sig))).astype(BF16)
+            sig = sigmoid(xf)
+            silu = xf * sig
+            out_ref[:, cols] = (zf * silu).astype(BF16)
+            gate_grad = (gf * zf * (sig + silu * (1.0 - sig))).astype(BF16)
             grad_ref[:, cols] = (back + gate_grad.astype(F32)).astype(BF16)
 
     block = pl.BlockSpec((size, step * plan.blk), lambda i: (start // size, i))
@@ -415,7 +424,7 @@
     before = 4 + 2 * count
     return call(
         kernel,
-        [me] + list(mixed) + list(grads) + [tokens, cotangent, first_t] + extra,
+        [me] + list(mixed) + list(grads) + [tokens, cotangent, in_hbm(first_t)] + extra,
         [SMEM]
         + arrivals(plan, size, step, inside)
         + arrivals(plan, size, step)
@@ -510,7 +519,7 @@
         out_ref[pl.ds(pl.multiple_of(side * half, half), half), :] = m_ref[...].astype(F32)
         out_ref[pl.ds(pl.multiple_of((1 - side) * half, half), half), :] = o_ref[...].astype(F32)
 
-    shape = jax.ShapeDtypeStruct((2 * half, cols), F32)
+    shape = pltpu.HBM((2 * half, cols), F32)
     return reorder(kernel, (place, mine, other), [shape], "join_halves", after)[0]
 
 
@@ -577,7 +586,7 @@
         sums["first"] = ran(first_term(plan, me, *args, after()))
 
     def do_mixed(start, length):
-        args = (plan, sums["u"], second_t, "own_mixed", start, length, after())
+        args = (plan, in_hbm(sums["u"]), second_t, "own_mixed", start, length, after())
         return ran(own_product(*args))
 
     def send_mixed(bufs, start, length, slot):
@@ -631,6 +640,11 @@
         do_grad_u(k, 2 * count + k - lead)
         if k + 1 < count:
             do_u(k + 1)
+        if k == count - 3:
+            do_u(k + 2)
+            break
+    for k in range(max(count - 2, 1), count):
+        do_grad_u(k, 2 * count - 1)
     second_grad = lax.psum(sums["second"], "dp")
     late = do_mixed(size, rows - size) if count > 1 else None
     early = do_mixed(0, size)

time: 236 us -> 232 us (0.983)
  Pallas kernels: 81.8 us -> 76.8 us
  waiting for transfers between devices: 67.5 us -> 71.3 us
    pallas_call x36, Pallas kernels: 81.8 us -> 76.8 us  [call(): pl.pallas_call(body, in_specs=list(in_specs) + [pl.BlockSpec(memory_space...]
    ppermute x50, waiting for transfers between devices: 60.6 us -> 63.1 us  [swap(): return lax.ppermute(value, axis, [(i, i ^ by) for i in range(size)])]
    unnamed x77 -> x73, local copies, waits for them, and re-layouts: 16 us -> 14.6 us
  transfers between devices with their start and end apart: 51 -> 51, of which waited for: 21 -> 23; matrix products, arithmetic and copies ran while one was open for 0% -> 0% of each run, Pallas kernels for 32% -> 31%
where the time goes in v2:
time: 232 us; the launch traced here: 231 us
  Pallas kernels  76.8 us (33%)
  waiting for transfers between devices  71.3 us (31%)
  starting transfers between devices  53.8 us (23%)
  local copies, waits for them, and re-layouts  14.6 us (6%)
  between operations  14.5 us (6%)
    pallas_call x36, Pallas kernels, call(): pl.pallas_call(body, in_specs=list(in_specs) + [pl.BlockSpec(memory_space...  76.8 us
    ppermute x50, waiting for transfers between devices, swap(): return lax.ppermute(value, axis, [(i, i ^ by) for i in range(size)])  63.1 us
    ppermute x50, starting transfers between devices, swap(): return lax.ppermute(value, axis, [(i, i ^ by) for i in range(size)])  53.8 us
    unnamed x73, local copies, waits for them, and re-layouts  14.6 us
    psum x1, waiting for transfers between devices, shards(): second_grad = lax.psum(sums['second'], 'dp')  8.21 us
  transfers between devices with their start and end apart: 51, of which 23 were waited for; matrix products, arithmetic and copies ran while one was open for 0% of the time, Pallas kernels for 31%

profile of v2, /device:TPU:0, one launch (start us, length us, event | category | flops | bytes accessed | tf_op | source)
XLA Modules:
  0.0 231.0 jit_solution(6098609099516250643)
XLA Ops:
  11.7 3.0 %collective-permute-start = (bf16[512,256]{1,0:T(8,128)(2,1)S(1)}, bf16[512,256]{1,0:T(8,128)(2,1)S(1)}, u32[]{:S(2)}, u32[]{:S(2)}) collective-permute-start(bf16[512,256]{1,0:T(8,128)(2,1)S(1)} %get-tuple-element.101), channel_id=1, source_target_pairs={{0,2},{1,3},{2,0},{3,1},{4,6},{5,7},{6,4},{7,5},{8,10},{9,11},{10,... | collective-permute-start | bytes 786440 | tf_op jit(solution)/shard_map/ppermute | solution.py:527
  23.9 3.6 %collective-permute-done.2.refs_3_.refs_2_ = bf16[512,256]{1,0:T(8,128)(2,1)S(1)} collective-permute-done((bf16[512,256]{1,0:T(8,128)(2,1)S(1)}, bf16[512,256]{1,0:T(8,128)(2,1)S(1)}, u32[]{:S(2)}, u32[]{:S(2)}) %collective-permute-start.2) | collective-permute-done | bytes 262176 | tf_op jit(solution)/shard_map/ppermute | solution.py:527
  27.5 5.2 %collective-permute-done.3.refs_4_.refs_3_ = bf16[512,256]{1,0:T(8,128)(2,1)S(1)} collective-permute-done((bf16[512,256]{1,0:T(8,128)(2,1)S(1)}, bf16[512,256]{1,0:T(8,128)(2,1)S(1)}, u32[]{:S(2)}, u32[]{:S(2)}) %collective-permute-start.3) | collective-permute-done | bytes 262176 | tf_op jit(solution)/shard_map/ppermute | solution.py:527
  33.2 2.9 %prepare_factors.1 = (bf16[16,128,128]{2,1,0:T(8,128)(2,1)S(1)}, bf16[16,128,128]{2,1,0:T(8,128)(2,1)S(1)}, bf16[16,128,128]{2,1,0:T(8,128)(2,1)S(1)}) custom-call(s32[1]{0:T(128)} %bitcast.refs_0_, bf16[16,128,128]{2,1,0:T(8,128)(2,1)S(1)} %copy-done.18, bf16[16,128,128]{2,1,0:T(8,128)(2,1)S(1)} %copy-done.19, ...), custom_call_target="tpu_custom_call" | custom-call | flops 268435456 | bytes 2621440 | tf_op jit(solution)/shard_map/prepare_factors/pallas_call | solution.py:128
  44.4 5.2 %collective-permute-done.8.refs_3_ = bf16[512,256]{1,0:T(8,128)(2,1)S(1)} collective-permute-done((bf16[512,256]{1,0:T(8,128)(2,1)S(1)}, bf16[512,256]{1,0:T(8,128)(2,1)S(1)}, u32[]{:S(2)}, u32[]{:S(2)}) %collective-permute-start.8) | collective-permute-done | bytes 262176 | tf_op jit(solution)/shard_map/ppermute | solution.py:527
  51.7 3.9 %collective-permute-done.4.refs_2_.refs_3_ = bf16[512,256]{1,0:T(8,128)(2,1)S(1)} collective-permute-done((bf16[512,256]{1,0:T(8,128)(2,1)S(1)}, bf16[512,256]{1,0:T(8,128)(2,1)S(1)}, u32[]{:S(2)}, u32[]{:S(2)}) %collective-permute-start.4) | collective-permute-done | bytes 262176 | tf_op jit(solution)/shard_map/ppermute | solution.py:527
  57.7 3.0 %collective-permute-done.5.refs_3_.refs_4_ = bf16[512,256]{1,0:T(8,128)(2,1)S(1)} collective-permute-done((bf16[512,256]{1,0:T(8,128)(2,1)S(1)}, bf16[512,256]{1,0:T(8,128)(2,1)S(1)}, u32[]{:S(2)}, u32[]{:S(2)}) %collective-permute-start.5) | collective-permute-done | bytes 262176 | tf_op jit(solution)/shard_map/ppermute | solution.py:527
  61.0 5.8 %collective-permute-done.9.refs_2_ = bf16[512,256]{1,0:T(8,128)(2,1)S(1)} collective-permute-done((bf16[512,256]{1,0:T(8,128)(2,1)S(1)}, bf16[512,256]{1,0:T(8,128)(2,1)S(1)}, u32[]{:S(2)}, u32[]{:S(2)}) %collective-permute-start.9) | collective-permute-done | bytes 262176 | tf_op jit(solution)/shard_map/ppermute | solution.py:527
  68.9 3.1 %collective-permute-done.10.refs_3_ = bf16[512,256]{1,0:T(8,128)(2,1)S(1)} collective-permute-done((bf16[512,256]{1,0:T(8,128)(2,1)S(1)}, bf16[512,256]{1,0:T(8,128)(2,1)S(1)}, u32[]{:S(2)}, u32[]{:S(2)}) %collective-permute-start.10) | collective-permute-done | bytes 262176 | tf_op jit(solution)/shard_map/ppermute | solution.py:527
  89.3 5.2 %collective-permute-done.19.refs_3_.refs_4_ = bf16[512,256]{1,0:T(8,128)(2,1)S(1)} collective-permute-done((bf16[512,256]{1,0:T(8,128)(2,1)S(1)}, bf16[512,256]{1,0:T(8,128)(2,1)S(1)}, u32[]{:S(2)}, u32[]{:S(2)}) %collective-permute-start.19) | collective-permute-done | bytes 262176 | tf_op jit(solution)/shard_map/ppermute | solution.py:527
  96.2 2.6 %own_grad_u.5 = (bf16[512,256]{1,0:T(8,128)(2,1)S(1)}, bf16[512,256]{1,0:T(8,128)(2,1)}, bf16[512,256]{1,0:T(8,128)(2,1)}, bf16[512,256]{1,0:T(8,128)(2,1)}) custom-call(bf16[16,128,256]{2,1,0:T(8,128)(2,1)S(1)} %own_grad_mixed.5.refs_4_.refs_5_.refs_0_, bf16[16,128,128]{2,1,0:T(8,128)(2,1)} %copy-done.5, ...), custom_call_target="tpu_custom_call" | custom-call | flops 402653184 | bytes 2097152 | tf_op jit(solution)/shard_map/own_grad_u/pallas_call | solution.py:128
  100.9 4.8 %collective-permute-done.15.refs_4_.refs_3_ = bf16[512,256]{1,0:T(8,128)(2,1)S(1)} collective-permute-done((bf16[512,256]{1,0:T(8,128)(2,1)S(1)}, bf16[512,256]{1,0:T(8,128)(2,1)S(1)}, u32[]{:S(2)}, u32[]{:S(2)}) %collective-permute-start.15) | collective-permute-done | bytes 262176 | tf_op jit(solution)/shard_map/ppermute | solution.py:527
  109.5 4.9 %own_u.7 = (bf16[16,128,1024]{2,1,0:T(8,128)(2,1)}, f32[16,128,128]{2,1,0:T(8,128)}) custom-call(s32[1]{0:T(128)} %bitcast.refs_0_, bf16[512,256]{1,0:T(8,128)(2,1)S(1)} %get-tuple-element.118.refs_4_.refs_1_, bf16[512,256]{1,0:T(8,128)(2,1)S(1)} %collective-permute-done.13.refs_2_, ...), custom_call_target="tpu_custom_call", output_to_operand_aliasing={{0}: (7, {})} | custom-call | flops 402653184 | bytes 3145728 | tf_op jit(solution)/shard_map/own_u/pallas_call | solution.py:128
  125.2 3.1 %collective-permute-done.32.refs_4_.refs_8_ = bf16[512,256]{1,0:T(8,128)(2,1)} collective-permute-done((bf16[512,256]{1,0:T(8,128)(2,1)}, bf16[512,256]{1,0:T(8,128)(2,1)}, u32[]{:S(2)}, u32[]{:S(2)}) %collective-permute-start.32) | collective-permute-done | bytes 262176 | tf_op jit(solution)/shard_map/ppermute | solution.py:527
  130.2 4.6 %own_mixed.2 = (bf16[512,768]{1,0:T(8,128)(2,1)S(1)}, bf16[512,768]{1,0:T(8,128)(2,1)S(1)}, bf16[512,768]{1,0:T(8,128)(2,1)S(1)}, bf16[512,768]{1,0:T(8,128)(2,1)S(1)}) custom-call(bf16[16,128,1024]{2,1,0:T(8,128)(2,1)} %get-tuple-element.139.refs_0_, bf16[16,128,128]{2,1,0:T(8,128)(2,1)} %copy-done.14, ...), custom_call_target="tpu_custom_call" | custom-call | flops 1207959552 | bytes 6291456 | tf_op jit(solution)/shard_map/own_mixed/pallas_call | solution.py:128
  136.7 2.7 %own_mixed.3 = (bf16[512,256]{1,0:T(8,128)(2,1)S(1)}, bf16[512,256]{1,0:T(8,128)(2,1)S(1)}, bf16[512,256]{1,0:T(8,128)(2,1)S(1)}, bf16[512,256]{1,0:T(8,128)(2,1)S(1)}) custom-call(bf16[16,128,1024]{2,1,0:T(8,128)(2,1)} %get-tuple-element.139.refs_0_, bf16[16,128,128]{2,1,0:T(8,128)(2,1)} %copy-done.14, bf16[512,768]{1,0:T(8,128)(2,1)S(1)} %get-tuple-element.144.refs_2_.refs_0_), custom_call_target="tpu_custom_call" | custom-call | flops 402653184 | bytes 2097152 | tf_op jit(solution)/shard_map/own_mixed/pallas_call | solution.py:128
  156.4 5.0 %first_term.7.refs_2_ = bf16[16,128,128]{2,1,0:T(8,128)(2,1)S(1)} custom-call(s32[1]{0:T(128)} %bitcast.refs_0_, bf16[512,256]{1,0:T(8,128)(2,1)} %copy-done.11, bf16[512,256]{1,0:T(8,128)(2,1)} %copy-done.31, bf16[512,256]{1,0:T(8,128)(2,1)} %copy-done.29, bf16[512,256]{1,0:T(8,128)(2,1)} %copy-done.30, bf16[1024,2048]{1,0:T(8,128)(2,1)} %refs_9_.7, ...), custom_call_target="tpu_custom_call" | custom-call | flops 134217728 | bytes 2097152 | tf_op jit(solution)/shard_map/first_term/pallas_call | solution.py:128
  163.2 6.9 %collective-permute-done.36.refs_2_ = bf16[1024,128]{1,0:T(8,128)(2,1)S(1)} collective-permute-done((bf16[1024,128]{1,0:T(8,128)(2,1)S(1)}, bf16[1024,128]{1,0:T(8,128)(2,1)S(1)}, u32[]{:S(2)}, u32[]{:S(2)}) %collective-permute-start.36) | collective-permute-done | bytes 262176 | tf_op jit(solution)/shard_map/ppermute | solution.py:527
  175.1 3.7 %collective-permute-start.45 = (bf16[256,128]{1,0:T(8,128)(2,1)S(1)}, bf16[256,128]{1,0:T(8,128)(2,1)S(1)}, u32[]{:S(2)}, u32[]{:S(2)}) collective-permute-start(bf16[256,128]{1,0:T(8,128)(2,1)S(1)} %get-tuple-element.177), channel_id=1, source_target_pairs={{0,24},{4,28},{8,16},{12,20},{16,8},{20,12},{24,0},{28,4},{1,25},{... | collective-permute-start | bytes 196616 | tf_op jit(solution)/shard_map/ppermute | solution.py:527
  190.4 4.3 %gate.4 = (bf16[1024,2048]{1,0:T(8,128)(2,1)}, bf16[1024,2048]{1,0:T(8,128)(2,1)}, f32[8,128]{1,0:T(8,128)S(1)}) custom-call(s32[1]{0:T(128)} %bitcast.refs_0_, bf16[512,768]{1,0:T(8,128)(2,1)} %get-tuple-element.164.refs_7_.refs_1_, bf16[512,768]{1,0:T(8,128)(2,1)} %copy-done.27, bf16[512,768]{1,0:T(8,128)(2,1)} %copy-done.28, ...), custom_call_target="tpu_custom_call" | custom-call | flops 268435456 | bytes 6291456 | tf_op jit(solution)/shard_map/gate/pallas_call | solution.py:128
  194.7 4.4 %gate.5 = (bf16[1024,2048]{1,0:T(8,128)(2,1)}, bf16[1024,2048]{1,0:T(8,128)(2,1)}, f32[8,128]{1,0:T(8,128)S(1)}) custom-call(s32[1]{0:T(128)} %bitcast.refs_0_, bf16[512,768]{1,0:T(8,128)(2,1)} %get-tuple-element.164.refs_7_.refs_1_, bf16[512,768]{1,0:T(8,128)(2,1)} %copy-done.27, ...), custom_call_target="tpu_custom_call", output_to_operand_aliasing={{0}: (12, {}), {1}: (13, {})} | custom-call | flops 268435456 | bytes 6291456 | tf_op jit(solution)/shard_map/gate/pallas_call | solution.py:128
  201.0 8.2 %all-reduce.2.cloned.1.call-done.refs_15_ = f32[16,128,128]{2,1,0:T(8,128)} async-done(((f32[16,128,128]{2,1,0:T(8,128)}), f32[16,128,128]{2,1,0:T(8,128)}) %all-reduce.2.cloned.1.call-update) | async-done | bytes 1048592 | tf_op jit(solution)/shard_map/psum | solution.py:648
  210.4 4.3 %gate.6 = (bf16[1024,2048]{1,0:T(8,128)(2,1)}, bf16[1024,2048]{1,0:T(8,128)(2,1)}, f32[8,128]{1,0:T(8,128)S(1)}) custom-call(s32[1]{0:T(128)} %bitcast.refs_0_, bf16[512,768]{1,0:T(8,128)(2,1)} %get-tuple-element.164.refs_7_.refs_1_, bf16[512,768]{1,0:T(8,128)(2,1)} %copy-done.27, ...), custom_call_target="tpu_custom_call", output_to_operand_aliasing={{0}: (12, {}), {1}: (13, {})} | custom-call | flops 268435456 | bytes 6291456 | tf_op jit(solution)/shard_map/gate/pallas_call | solution.py:128
  217.0 4.4 %gate.7 = (bf16[1024,2048]{1,0:T(8,128)(2,1)}, bf16[1024,2048]{1,0:T(8,128)(2,1)}, f32[8,128]{1,0:T(8,128)S(1)}) custom-call(s32[1]{0:T(128)} %bitcast.refs_0_, bf16[512,256]{1,0:T(8,128)(2,1)} %get-tuple-element.168.refs_5_.refs_1_, bf16[512,256]{1,0:T(8,128)(2,1)} %copy-done.33, ...), custom_call_target="tpu_custom_call", output_to_operand_aliasing={{0}: (12, {}), {1}: (13, {})} | custom-call | flops 268435456 | bytes 6291456 | tf_op jit(solution)/shard_map/gate/pallas_call | solution.py:128
  (190 shorter events, 111.6 us)
Async XLA Ops:
  15.6 24.6 %collective-permute-start.1 = (bf16[512,256]{1,0:T(8,128)(2,1)S(1)}, bf16[512,256]{1,0:T(8,128)(2,1)S(1)}, u32[]{:S(2)}, u32[]{:S(2)}) collective-permute-start(bf16[512,256]{1,0:T(8,128)(2,1)S(1)} %get-tuple-element.102), channel_id=1, source_target_pairs={{0,3},{1,2},{2,1},{3,0},{4,7},{5,6},{6,5},{7,4},{8,11},{9,10},{10,... | collective-permute-start | bytes 786440 | tf_op jit(solution)/shard_map/ppermute | solution.py:527
  18.9 23.1 %collective-permute-start.6 = (bf16[512,256]{1,0:T(8,128)(2,1)S(1)}, bf16[512,256]{1,0:T(8,128)(2,1)S(1)}, u32[]{:S(2)}, u32[]{:S(2)}) collective-permute-start(bf16[512,256]{1,0:T(8,128)(2,1)S(1)} %get-tuple-element.108), channel_id=1, source_target_pairs={{0,1},{1,0},{2,3},{3,2},{4,5},{5,4},{6,7},{7,6},{8,9},{9,8},{10,11... | collective-permute-start | bytes 786440 | tf_op jit(solution)/shard_map/ppermute | solution.py:527
  21.9 22.5 %collective-permute-start.7 = (bf16[512,256]{1,0:T(8,128)(2,1)S(1)}, bf16[512,256]{1,0:T(8,128)(2,1)S(1)}, u32[]{:S(2)}, u32[]{:S(2)}) collective-permute-start(bf16[512,256]{1,0:T(8,128)(2,1)S(1)} %get-tuple-element.109), channel_id=1, source_target_pairs={{0,2},{1,3},{2,0},{3,1},{4,6},{5,7},{6,4},{7,5},{8,10},{9,11},{10,... | collective-permute-start | bytes 786440 | tf_op jit(solution)/shard_map/ppermute | solution.py:527
  27.5 22.0 %collective-permute-start.8 = (bf16[512,256]{1,0:T(8,128)(2,1)S(1)}, bf16[512,256]{1,0:T(8,128)(2,1)S(1)}, u32[]{:S(2)}, u32[]{:S(2)}) collective-permute-start(bf16[512,256]{1,0:T(8,128)(2,1)S(1)} %get-tuple-element.110), channel_id=1, source_target_pairs={{0,3},{1,2},{2,1},{3,0},{4,7},{5,6},{6,5},{7,4},{8,11},{9,10},{10,... | collective-permute-start | bytes 786440 | tf_op jit(solution)/shard_map/ppermute | solution.py:527
  49.7 22.3 %collective-permute-start.10 = (bf16[512,256]{1,0:T(8,128)(2,1)S(1)}, bf16[512,256]{1,0:T(8,128)(2,1)S(1)}, u32[]{:S(2)}, u32[]{:S(2)}) collective-permute-start(bf16[512,256]{1,0:T(8,128)(2,1)S(1)} %get-tuple-element.112), channel_id=1, source_target_pairs={{0,3},{1,2},{2,1},{3,0},{4,7},{5,6},{6,5},{7,4},{8,11},{9,10},{10,... | collective-permute-start | bytes 786440 | tf_op jit(solution)/shard_map/ppermute | solution.py:527
  51.5 24.6 %collective-permute-start.16 = (bf16[512,256]{1,0:T(8,128)(2,1)S(1)}, bf16[512,256]{1,0:T(8,128)(2,1)S(1)}, u32[]{:S(2)}, u32[]{:S(2)}) collective-permute-start(bf16[512,256]{1,0:T(8,128)(2,1)S(1)} %get-tuple-element.122), channel_id=1, source_target_pairs={{0,1},{1,0},{2,3},{3,2},{4,5},{5,4},{6,7},{7,6},{8,9},{9,8},{10,11... | collective-permute-start | bytes 786440 | tf_op jit(solution)/shard_map/ppermute | solution.py:527
  55.6 20.6 %collective-permute-start.23 = (bf16[512,256]{1,0:T(8,128)(2,1)S(1)}, bf16[512,256]{1,0:T(8,128)(2,1)S(1)}, u32[]{:S(2)}, u32[]{:S(2)}) collective-permute-start(bf16[512,256]{1,0:T(8,128)(2,1)S(1)} %get-tuple-element.129), channel_id=1, source_target_pairs={{0,1},{1,0},{2,3},{3,2},{4,5},{5,4},{6,7},{7,6},{8,9},{9,8},{10,11... | collective-permute-start | bytes 786440 | tf_op jit(solution)/shard_map/ppermute | solution.py:527
  60.8 19.7 %collective-permute-start.20 = (bf16[512,256]{1,0:T(8,128)(2,1)S(1)}, bf16[512,256]{1,0:T(8,128)(2,1)S(1)}, u32[]{:S(2)}, u32[]{:S(2)}) collective-permute-start(bf16[512,256]{1,0:T(8,128)(2,1)S(1)} %get-tuple-element.126), channel_id=1, source_target_pairs={{0,1},{1,0},{2,3},{3,2},{4,5},{5,4},{6,7},{7,6},{8,9},{9,8},{10,11... | collective-permute-start | bytes 786440 | tf_op jit(solution)/shard_map/ppermute | solution.py:527
  82.5 18.4 %collective-permute-start.14 = (bf16[512,256]{1,0:T(8,128)(2,1)S(1)}, bf16[512,256]{1,0:T(8,128)(2,1)S(1)}, u32[]{:S(2)}, u32[]{:S(2)}) collective-permute-start(bf16[512,256]{1,0:T(8,128)(2,1)S(1)} %get-tuple-element.120), channel_id=1, source_target_pairs={{0,2},{1,3},{2,0},{3,1},{4,6},{5,7},{6,4},{7,5},{8,10},{9,11},{10,... | collective-permute-start | bytes 786440 | tf_op jit(solution)/shard_map/ppermute | solution.py:527
  83.3 22.5 %collective-permute-start.15 = (bf16[512,256]{1,0:T(8,128)(2,1)S(1)}, bf16[512,256]{1,0:T(8,128)(2,1)S(1)}, u32[]{:S(2)}, u32[]{:S(2)}) collective-permute-start(bf16[512,256]{1,0:T(8,128)(2,1)S(1)} %get-tuple-element.121), channel_id=1, source_target_pairs={{0,3},{1,2},{2,1},{3,0},{4,7},{5,6},{6,5},{7,4},{8,11},{9,10},{10,... | collective-permute-start | bytes 786440 | tf_op jit(solution)/shard_map/ppermute | solution.py:527
  108.0 20.3 %collective-permute-start.32 = (bf16[512,256]{1,0:T(8,128)(2,1)}, bf16[512,256]{1,0:T(8,128)(2,1)}, u32[]{:S(2)}, u32[]{:S(2)}) collective-permute-start(bf16[512,256]{1,0:T(8,128)(2,1)} %get-tuple-element.157), channel_id=1, source_target_pairs={{0,3},{1,2},{2,1},{3,0},{4,7},{5,6},{6,5},{7,4},{8,11},{9,10},{10,... | collective-permute-start | bytes 786440 | tf_op jit(solution)/shard_map/ppermute | solution.py:527
  116.9 92.2 %all-reduce.2.cloned.1.call-start = ((), (), s32[]{:S(2)}) async-start(), calls=%async_computation | async-start | bytes 2097152 | tf_op jit(solution)/shard_map/psum | solution.py:648
  116.9 28.1 %collective-permute-start.27 = (bf16[512,256]{1,0:T(8,128)(2,1)}, bf16[512,256]{1,0:T(8,128)(2,1)}, u32[]{:S(2)}, u32[]{:S(2)}) collective-permute-start(bf16[512,256]{1,0:T(8,128)(2,1)} %copy-done.26), channel_id=1, source_target_pairs={{0,1},{1,0},{2,3},{3,2},{4,5},{5,4},{6,7},{7,6},{8,9},{9,8},{10,11... | collective-permute-start | bytes 786440 | tf_op jit(solution)/shard_map/ppermute | solution.py:527
  117.2 27.8 %collective-permute-start.28 = (bf16[512,256]{1,0:T(8,128)(2,1)S(1)}, bf16[512,256]{1,0:T(8,128)(2,1)}, u32[]{:S(2)}, u32[]{:S(2)}) collective-permute-start(bf16[512,256]{1,0:T(8,128)(2,1)S(1)} %get-tuple-element.153), channel_id=1, source_target_pairs={{0,2},{1,3},{2,0},{3,1},{4,6},{5,7},{6,4},{7,5},{8,10},{9,11},{10,... | collective-permute-start | bytes 786440 | tf_op jit(solution)/shard_map/ppermute | solution.py:527
  119.1 25.9 %collective-permute-start.29 = (bf16[512,256]{1,0:T(8,128)(2,1)S(1)}, bf16[512,256]{1,0:T(8,128)(2,1)}, u32[]{:S(2)}, u32[]{:S(2)}) collective-permute-start(bf16[512,256]{1,0:T(8,128)(2,1)S(1)} %get-tuple-element.154), channel_id=1, source_target_pairs={{0,3},{1,2},{2,1},{3,0},{4,7},{5,6},{6,5},{7,4},{8,11},{9,10},{10,... | collective-permute-start | bytes 786440 | tf_op jit(solution)/shard_map/ppermute | solution.py:527
  123.1 24.9 %collective-permute-start.25 = (bf16[512,256]{1,0:T(8,128)(2,1)}, bf16[512,256]{1,0:T(8,128)(2,1)S(1)}, u32[]{:S(2)}, u32[]{:S(2)}) collective-permute-start(bf16[512,256]{1,0:T(8,128)(2,1)} %get-tuple-element.150), channel_id=1, source_target_pairs={{0,2},{1,3},{2,0},{3,1},{4,6},{5,7},{6,4},{7,5},{8,10},{9,11},{10,... | collective-permute-start | bytes 786440 | tf_op jit(solution)/shard_map/ppermute | solution.py:527
  128.3 21.2 %collective-permute-start.26 = (bf16[512,256]{1,0:T(8,128)(2,1)S(1)}, bf16[512,256]{1,0:T(8,128)(2,1)S(1)}, u32[]{:S(2)}, u32[]{:S(2)}) collective-permute-start(bf16[512,256]{1,0:T(8,128)(2,1)S(1)} %get-tuple-element.151), channel_id=1, source_target_pairs={{0,3},{1,2},{2,1},{3,0},{4,7},{5,6},{6,5},{7,4},{8,11},{9,10},{10,... | collective-permute-start | bytes 786440 | tf_op jit(solution)/shard_map/ppermute | solution.py:527
  150.2 35.1 %collective-permute-start.40 = (bf16[512,768]{1,0:T(8,128)(2,1)}, bf16[512,768]{1,0:T(8,128)(2,1)S(1)}, u32[]{:S(2)}, u32[]{:S(2)}) collective-permute-start(bf16[512,768]{1,0:T(8,128)(2,1)} %get-tuple-element.172), channel_id=1, source_target_pairs={{0,1},{1,0},{2,3},{3,2},{4,5},{5,4},{6,7},{7,6},{8,9},{9,8},{10,11... | collective-permute-start | bytes 2359304 | tf_op jit(solution)/shard_map/ppermute | solution.py:527
  151.2 35.8 %collective-permute-start.41 = (bf16[512,768]{1,0:T(8,128)(2,1)}, bf16[512,768]{1,0:T(8,128)(2,1)S(1)}, u32[]{:S(2)}, u32[]{:S(2)}) collective-permute-start(bf16[512,768]{1,0:T(8,128)(2,1)} %get-tuple-element.173), channel_id=1, source_target_pairs={{0,2},{1,3},{2,0},{3,1},{4,6},{5,7},{6,4},{7,5},{8,10},{9,11},{10,... | collective-permute-start | bytes 2359304 | tf_op jit(solution)/shard_map/ppermute | solution.py:527
  152.9 36.2 %collective-permute-start.42 = (bf16[512,768]{1,0:T(8,128)(2,1)}, bf16[512,768]{1,0:T(8,128)(2,1)}, u32[]{:S(2)}, u32[]{:S(2)}) collective-permute-start(bf16[512,768]{1,0:T(8,128)(2,1)} %get-tuple-element.174), channel_id=1, source_target_pairs={{0,3},{1,2},{2,1},{3,0},{4,7},{5,6},{6,5},{7,4},{8,11},{9,10},{10,... | collective-permute-start | bytes 2359304 | tf_op jit(solution)/shard_map/ppermute | solution.py:527
  185.4 30.7 %collective-permute-start.37 = (bf16[512,256]{1,0:T(8,128)(2,1)}, bf16[512,256]{1,0:T(8,128)(2,1)S(1)}, u32[]{:S(2)}, u32[]{:S(2)}) collective-permute-start(bf16[512,256]{1,0:T(8,128)(2,1)} %get-tuple-element.169), channel_id=1, source_target_pairs={{0,1},{1,0},{2,3},{3,2},{4,5},{5,4},{6,7},{7,6},{8,9},{9,8},{10,11... | collective-permute-start | bytes 786440 | tf_op jit(solution)/shard_map/ppermute | solution.py:527
  185.4 30.7 %collective-permute-start.38 = (bf16[512,256]{1,0:T(8,128)(2,1)}, bf16[512,256]{1,0:T(8,128)(2,1)S(1)}, u32[]{:S(2)}, u32[]{:S(2)}) collective-permute-start(bf16[512,256]{1,0:T(8,128)(2,1)} %get-tuple-element.170), channel_id=1, source_target_pairs={{0,2},{1,3},{2,0},{3,1},{4,6},{5,7},{6,4},{7,5},{8,10},{9,11},{10,... | collective-permute-start | bytes 786440 | tf_op jit(solution)/shard_map/ppermute | solution.py:527
  187.0 27.7 %collective-permute-start.47 = (bf16[256,128]{1,0:T(8,128)(2,1)S(1)}, bf16[256,128]{1,0:T(8,128)(2,1)S(1)}, u32[]{:S(2)}, u32[]{:S(2)}) collective-permute-start(bf16[256,128]{1,0:T(8,128)(2,1)S(1)} %add_up.1.refs_12_.refs_1_), channel_id=1, source_target_pairs={{0,16},{4,20},{8,24},{12,28},{16,0},{20,4},{24,8},{28,12},{1,17},{... | collective-permute-start | bytes 196616 | tf_op jit(solution)/shard_map/ppermute | solution.py:527
  189.1 25.6 %collective-permute-start.48 = (bf16[256,128]{1,0:T(8,128)(2,1)S(1)}, bf16[256,128]{1,0:T(8,128)(2,1)S(1)}, u32[]{:S(2)}, u32[]{:S(2)}) collective-permute-start(bf16[256,128]{1,0:T(8,128)(2,1)S(1)} %add_up.1.refs_12_.refs_1_), channel_id=1, source_target_pairs={{0,24},{4,28},{8,16},{12,20},{16,8},{20,12},{24,0},{28,4},{1,25},{... | collective-permute-start | bytes 196616 | tf_op jit(solution)/shard_map/ppermute | solution.py:527
  (63 other events, 558.5 us)
Sparse Core Ops, SparseCore 0:
  130.4 78.7 all-reduce.1

commit v3 on v2

--- a/solution.py
+++ b/solution.py
@@ -298,11 +298,8 @@
             if extra:
                 term = term + refs[2 + count][j]
             if scale is not None:
-                term = term * scale
-                high = term.astype(BF16)
-                low = (term - high.astype(F32)).astype(BF16)
-                high = dot(dot(order, high, TN).astype(BF16), rel, NN)
-                term = high + dot(dot(order, low, TN).astype(BF16), rel, NN)
+                term = dot(order, (term * scale).astype(BF16), TN).astype(BF16)
+                term = dot(term, rel, NN)
             sum_ref[j] = term
 
     return call(

time: 232 us -> 232 us (level)
  transfers between devices with their start and end apart: 51 -> 51, of which waited for: 23 -> 24; matrix products, arithmetic and copies ran while one was open for 0% -> 0% of each run, Pallas kernels for 31% -> 30%
where the time goes in v3:
time: 232 us; the launch traced here: 231 us
  Pallas kernels  75.6 us (33%)
  waiting for transfers between devices  72.4 us (31%)
  starting transfers between devices  53.8 us (23%)
  local copies, waits for them, and re-layouts  14.6 us (6%)
  between operations  14.5 us (6%)
    pallas_call x36, Pallas kernels, call(): pl.pallas_call(body, in_specs=list(in_specs) + [pl.BlockSpec(memory_space...  75.6 us
    ppermute x50, waiting for transfers between devices, swap(): return lax.ppermute(value, axis, [(i, i ^ by) for i in range(size)])  64.2 us
    ppermute x50, starting transfers between devices, swap(): return lax.ppermute(value, axis, [(i, i ^ by) for i in range(size)])  53.8 us
    unnamed x73, local copies, waits for them, and re-layouts  14.6 us
    psum x1, waiting for transfers between devices, shards(): second_grad = lax.psum(sums['second'], 'dp')  8.21 us
  transfers between devices with their start and end apart: 51, of which 24 were waited for; matrix products, arithmetic and copies ran while one was open for 0% of the time, Pallas kernels for 30%

profile of v3, /device:TPU:0, one launch (start us, length us, event | category | flops | bytes accessed | tf_op | source)
XLA Modules:
  0.0 231.0 jit_solution(17474874604889696681)
XLA Ops:
  11.7 3.0 %collective-permute-start = (bf16[512,256]{1,0:T(8,128)(2,1)S(1)}, bf16[512,256]{1,0:T(8,128)(2,1)S(1)}, u32[]{:S(2)}, u32[]{:S(2)}) collective-permute-start(bf16[512,256]{1,0:T(8,128)(2,1)S(1)} %get-tuple-element.101), channel_id=1, source_target_pairs={{0,2},{1,3},{2,0},{3,1},{4,6},{5,7},{6,4},{7,5},{8,10},{9,11},{10,... | collective-permute-start | bytes 786440 | tf_op jit(solution)/shard_map/ppermute | solution.py:524
  23.9 3.6 %collective-permute-done.2.refs_3_.refs_2_ = bf16[512,256]{1,0:T(8,128)(2,1)S(1)} collective-permute-done((bf16[512,256]{1,0:T(8,128)(2,1)S(1)}, bf16[512,256]{1,0:T(8,128)(2,1)S(1)}, u32[]{:S(2)}, u32[]{:S(2)}) %collective-permute-start.2) | collective-permute-done | bytes 262176 | tf_op jit(solution)/shard_map/ppermute | solution.py:524
  27.5 5.2 %collective-permute-done.3.refs_4_.refs_3_ = bf16[512,256]{1,0:T(8,128)(2,1)S(1)} collective-permute-done((bf16[512,256]{1,0:T(8,128)(2,1)S(1)}, bf16[512,256]{1,0:T(8,128)(2,1)S(1)}, u32[]{:S(2)}, u32[]{:S(2)}) %collective-permute-start.3) | collective-permute-done | bytes 262176 | tf_op jit(solution)/shard_map/ppermute | solution.py:524
  33.2 2.9 %prepare_factors.1 = (bf16[16,128,128]{2,1,0:T(8,128)(2,1)S(1)}, bf16[16,128,128]{2,1,0:T(8,128)(2,1)S(1)}, bf16[16,128,128]{2,1,0:T(8,128)(2,1)S(1)}) custom-call(s32[1]{0:T(128)} %bitcast.refs_0_, bf16[16,128,128]{2,1,0:T(8,128)(2,1)S(1)} %copy-done.18, bf16[16,128,128]{2,1,0:T(8,128)(2,1)S(1)} %copy-done.19, ...), custom_call_target="tpu_custom_call" | custom-call | flops 268435456 | bytes 2621440 | tf_op jit(solution)/shard_map/prepare_factors/pallas_call | solution.py:128
  44.4 5.2 %collective-permute-done.8.refs_3_ = bf16[512,256]{1,0:T(8,128)(2,1)S(1)} collective-permute-done((bf16[512,256]{1,0:T(8,128)(2,1)S(1)}, bf16[512,256]{1,0:T(8,128)(2,1)S(1)}, u32[]{:S(2)}, u32[]{:S(2)}) %collective-permute-start.8) | collective-permute-done | bytes 262176 | tf_op jit(solution)/shard_map/ppermute | solution.py:524
  51.7 3.9 %collective-permute-done.4.refs_2_.refs_3_ = bf16[512,256]{1,0:T(8,128)(2,1)S(1)} collective-permute-done((bf16[512,256]{1,0:T(8,128)(2,1)S(1)}, bf16[512,256]{1,0:T(8,128)(2,1)S(1)}, u32[]{:S(2)}, u32[]{:S(2)}) %collective-permute-start.4) | collective-permute-done | bytes 262176 | tf_op jit(solution)/shard_map/ppermute | solution.py:524
  57.7 3.0 %collective-permute-done.5.refs_3_.refs_4_ = bf16[512,256]{1,0:T(8,128)(2,1)S(1)} collective-permute-done((bf16[512,256]{1,0:T(8,128)(2,1)S(1)}, bf16[512,256]{1,0:T(8,128)(2,1)S(1)}, u32[]{:S(2)}, u32[]{:S(2)}) %collective-permute-start.5) | collective-permute-done | bytes 262176 | tf_op jit(solution)/shard_map/ppermute | solution.py:524
  61.0 5.8 %collective-permute-done.9.refs_2_ = bf16[512,256]{1,0:T(8,128)(2,1)S(1)} collective-permute-done((bf16[512,256]{1,0:T(8,128)(2,1)S(1)}, bf16[512,256]{1,0:T(8,128)(2,1)S(1)}, u32[]{:S(2)}, u32[]{:S(2)}) %collective-permute-start.9) | collective-permute-done | bytes 262176 | tf_op jit(solution)/shard_map/ppermute | solution.py:524
  68.9 3.1 %collective-permute-done.10.refs_3_ = bf16[512,256]{1,0:T(8,128)(2,1)S(1)} collective-permute-done((bf16[512,256]{1,0:T(8,128)(2,1)S(1)}, bf16[512,256]{1,0:T(8,128)(2,1)S(1)}, u32[]{:S(2)}, u32[]{:S(2)}) %collective-permute-start.10) | collective-permute-done | bytes 262176 | tf_op jit(solution)/shard_map/ppermute | solution.py:524
  89.3 5.2 %collective-permute-done.19.refs_3_.refs_4_ = bf16[512,256]{1,0:T(8,128)(2,1)S(1)} collective-permute-done((bf16[512,256]{1,0:T(8,128)(2,1)S(1)}, bf16[512,256]{1,0:T(8,128)(2,1)S(1)}, u32[]{:S(2)}, u32[]{:S(2)}) %collective-permute-start.19) | collective-permute-done | bytes 262176 | tf_op jit(solution)/shard_map/ppermute | solution.py:524
  96.2 2.6 %own_grad_u.5 = (bf16[512,256]{1,0:T(8,128)(2,1)S(1)}, bf16[512,256]{1,0:T(8,128)(2,1)}, bf16[512,256]{1,0:T(8,128)(2,1)}, bf16[512,256]{1,0:T(8,128)(2,1)}) custom-call(bf16[16,128,256]{2,1,0:T(8,128)(2,1)S(1)} %own_grad_mixed.5.refs_4_.refs_5_.refs_0_, bf16[16,128,128]{2,1,0:T(8,128)(2,1)} %copy-done.5, ...), custom_call_target="tpu_custom_call" | custom-call | flops 402653184 | bytes 2097152 | tf_op jit(solution)/shard_map/own_grad_u/pallas_call | solution.py:128
  100.9 4.8 %collective-permute-done.15.refs_4_.refs_3_ = bf16[512,256]{1,0:T(8,128)(2,1)S(1)} collective-permute-done((bf16[512,256]{1,0:T(8,128)(2,1)S(1)}, bf16[512,256]{1,0:T(8,128)(2,1)S(1)}, u32[]{:S(2)}, u32[]{:S(2)}) %collective-permute-start.15) | collective-permute-done | bytes 262176 | tf_op jit(solution)/shard_map/ppermute | solution.py:524
  109.5 3.8 %own_u.7 = (bf16[16,128,1024]{2,1,0:T(8,128)(2,1)}, f32[16,128,128]{2,1,0:T(8,128)}) custom-call(s32[1]{0:T(128)} %bitcast.refs_0_, bf16[512,256]{1,0:T(8,128)(2,1)S(1)} %get-tuple-element.118.refs_4_.refs_1_, bf16[512,256]{1,0:T(8,128)(2,1)S(1)} %collective-permute-done.13.refs_2_, ...), custom_call_target="tpu_custom_call", output_to_operand_aliasing={{0}: (7, {})} | custom-call | flops 402653184 | bytes 3145728 | tf_op jit(solution)/shard_map/own_u/pallas_call | solution.py:128
  125.2 3.1 %collective-permute-done.32.refs_4_.refs_8_ = bf16[512,256]{1,0:T(8,128)(2,1)} collective-permute-done((bf16[512,256]{1,0:T(8,128)(2,1)}, bf16[512,256]{1,0:T(8,128)(2,1)}, u32[]{:S(2)}, u32[]{:S(2)}) %collective-permute-start.32) | collective-permute-done | bytes 262176 | tf_op jit(solution)/shard_map/ppermute | solution.py:524
  130.2 4.6 %own_mixed.2 = (bf16[512,768]{1,0:T(8,128)(2,1)S(1)}, bf16[512,768]{1,0:T(8,128)(2,1)S(1)}, bf16[512,768]{1,0:T(8,128)(2,1)S(1)}, bf16[512,768]{1,0:T(8,128)(2,1)S(1)}) custom-call(bf16[16,128,1024]{2,1,0:T(8,128)(2,1)} %get-tuple-element.139.refs_0_, bf16[16,128,128]{2,1,0:T(8,128)(2,1)} %copy-done.14, ...), custom_call_target="tpu_custom_call" | custom-call | flops 1207959552 | bytes 6291456 | tf_op jit(solution)/shard_map/own_mixed/pallas_call | solution.py:128
  136.7 2.7 %own_mixed.3 = (bf16[512,256]{1,0:T(8,128)(2,1)S(1)}, bf16[512,256]{1,0:T(8,128)(2,1)S(1)}, bf16[512,256]{1,0:T(8,128)(2,1)S(1)}, bf16[512,256]{1,0:T(8,128)(2,1)S(1)}) custom-call(bf16[16,128,1024]{2,1,0:T(8,128)(2,1)} %get-tuple-element.139.refs_0_, bf16[16,128,128]{2,1,0:T(8,128)(2,1)} %copy-done.14, bf16[512,768]{1,0:T(8,128)(2,1)S(1)} %get-tuple-element.144.refs_2_.refs_0_), custom_call_target="tpu_custom_call" | custom-call | flops 402653184 | bytes 2097152 | tf_op jit(solution)/shard_map/own_mixed/pallas_call | solution.py:128
  156.4 5.0 %first_term.7.refs_2_ = bf16[16,128,128]{2,1,0:T(8,128)(2,1)S(1)} custom-call(s32[1]{0:T(128)} %bitcast.refs_0_, bf16[512,256]{1,0:T(8,128)(2,1)} %copy-done.11, bf16[512,256]{1,0:T(8,128)(2,1)} %copy-done.31, bf16[512,256]{1,0:T(8,128)(2,1)} %copy-done.29, bf16[512,256]{1,0:T(8,128)(2,1)} %copy-done.30, bf16[1024,2048]{1,0:T(8,128)(2,1)} %refs_9_.7, ...), custom_call_target="tpu_custom_call" | custom-call | flops 134217728 | bytes 2097152 | tf_op jit(solution)/shard_map/first_term/pallas_call | solution.py:128
  163.2 6.9 %collective-permute-done.36.refs_2_ = bf16[1024,128]{1,0:T(8,128)(2,1)S(1)} collective-permute-done((bf16[1024,128]{1,0:T(8,128)(2,1)S(1)}, bf16[1024,128]{1,0:T(8,128)(2,1)S(1)}, u32[]{:S(2)}, u32[]{:S(2)}) %collective-permute-start.36) | collective-permute-done | bytes 262176 | tf_op jit(solution)/shard_map/ppermute | solution.py:524
  175.1 3.7 %collective-permute-start.45 = (bf16[256,128]{1,0:T(8,128)(2,1)S(1)}, bf16[256,128]{1,0:T(8,128)(2,1)S(1)}, u32[]{:S(2)}, u32[]{:S(2)}) collective-permute-start(bf16[256,128]{1,0:T(8,128)(2,1)S(1)} %get-tuple-element.177), channel_id=1, source_target_pairs={{0,24},{4,28},{8,16},{12,20},{16,8},{20,12},{24,0},{28,4},{1,25},{... | collective-permute-start | bytes 196616 | tf_op jit(solution)/shard_map/ppermute | solution.py:524
  190.4 4.3 %gate.4 = (bf16[1024,2048]{1,0:T(8,128)(2,1)}, bf16[1024,2048]{1,0:T(8,128)(2,1)}, f32[8,128]{1,0:T(8,128)S(1)}) custom-call(s32[1]{0:T(128)} %bitcast.refs_0_, bf16[512,768]{1,0:T(8,128)(2,1)} %get-tuple-element.164.refs_7_.refs_1_, bf16[512,768]{1,0:T(8,128)(2,1)} %copy-done.27, bf16[512,768]{1,0:T(8,128)(2,1)} %copy-done.28, ...), custom_call_target="tpu_custom_call" | custom-call | flops 268435456 | bytes 6291456 | tf_op jit(solution)/shard_map/gate/pallas_call | solution.py:128
  194.7 4.4 %gate.5 = (bf16[1024,2048]{1,0:T(8,128)(2,1)}, bf16[1024,2048]{1,0:T(8,128)(2,1)}, f32[8,128]{1,0:T(8,128)S(1)}) custom-call(s32[1]{0:T(128)} %bitcast.refs_0_, bf16[512,768]{1,0:T(8,128)(2,1)} %get-tuple-element.164.refs_7_.refs_1_, bf16[512,768]{1,0:T(8,128)(2,1)} %copy-done.27, ...), custom_call_target="tpu_custom_call", output_to_operand_aliasing={{0}: (12, {}), {1}: (13, {})} | custom-call | flops 268435456 | bytes 6291456 | tf_op jit(solution)/shard_map/gate/pallas_call | solution.py:128
  201.0 8.2 %all-reduce.2.cloned.1.call-done.refs_15_ = f32[16,128,128]{2,1,0:T(8,128)} async-done(((f32[16,128,128]{2,1,0:T(8,128)}), f32[16,128,128]{2,1,0:T(8,128)}) %all-reduce.2.cloned.1.call-update) | async-done | bytes 1048592 | tf_op jit(solution)/shard_map/psum | solution.py:645
  210.4 4.3 %gate.6 = (bf16[1024,2048]{1,0:T(8,128)(2,1)}, bf16[1024,2048]{1,0:T(8,128)(2,1)}, f32[8,128]{1,0:T(8,128)S(1)}) custom-call(s32[1]{0:T(128)} %bitcast.refs_0_, bf16[512,768]{1,0:T(8,128)(2,1)} %get-tuple-element.164.refs_7_.refs_1_, bf16[512,768]{1,0:T(8,128)(2,1)} %copy-done.27, ...), custom_call_target="tpu_custom_call", output_to_operand_aliasing={{0}: (12, {}), {1}: (13, {})} | custom-call | flops 268435456 | bytes 6291456 | tf_op jit(solution)/shard_map/gate/pallas_call | solution.py:128
  217.0 4.4 %gate.7 = (bf16[1024,2048]{1,0:T(8,128)(2,1)}, bf16[1024,2048]{1,0:T(8,128)(2,1)}, f32[8,128]{1,0:T(8,128)S(1)}) custom-call(s32[1]{0:T(128)} %bitcast.refs_0_, bf16[512,256]{1,0:T(8,128)(2,1)} %get-tuple-element.168.refs_5_.refs_1_, bf16[512,256]{1,0:T(8,128)(2,1)} %copy-done.33, ...), custom_call_target="tpu_custom_call", output_to_operand_aliasing={{0}: (12, {}), {1}: (13, {})} | custom-call | flops 268435456 | bytes 6291456 | tf_op jit(solution)/shard_map/gate/pallas_call | solution.py:128
  (190 shorter events, 112.7 us)
Async XLA Ops:
  15.6 24.6 %collective-permute-start.1 = (bf16[512,256]{1,0:T(8,128)(2,1)S(1)}, bf16[512,256]{1,0:T(8,128)(2,1)S(1)}, u32[]{:S(2)}, u32[]{:S(2)}) collective-permute-start(bf16[512,256]{1,0:T(8,128)(2,1)S(1)} %get-tuple-element.102), channel_id=1, source_target_pairs={{0,3},{1,2},{2,1},{3,0},{4,7},{5,6},{6,5},{7,4},{8,11},{9,10},{10,... | collective-permute-start | bytes 786440 | tf_op jit(solution)/shard_map/ppermute | solution.py:524
  18.9 23.1 %collective-permute-start.6 = (bf16[512,256]{1,0:T(8,128)(2,1)S(1)}, bf16[512,256]{1,0:T(8,128)(2,1)S(1)}, u32[]{:S(2)}, u32[]{:S(2)}) collective-permute-start(bf16[512,256]{1,0:T(8,128)(2,1)S(1)} %get-tuple-element.108), channel_id=1, source_target_pairs={{0,1},{1,0},{2,3},{3,2},{4,5},{5,4},{6,7},{7,6},{8,9},{9,8},{10,11... | collective-permute-start | bytes 786440 | tf_op jit(solution)/shard_map/ppermute | solution.py:524
  21.9 22.5 %collective-permute-start.7 = (bf16[512,256]{1,0:T(8,128)(2,1)S(1)}, bf16[512,256]{1,0:T(8,128)(2,1)S(1)}, u32[]{:S(2)}, u32[]{:S(2)}) collective-permute-start(bf16[512,256]{1,0:T(8,128)(2,1)S(1)} %get-tuple-element.109), channel_id=1, source_target_pairs={{0,2},{1,3},{2,0},{3,1},{4,6},{5,7},{6,4},{7,5},{8,10},{9,11},{10,... | collective-permute-start | bytes 786440 | tf_op jit(solution)/shard_map/ppermute | solution.py:524
  27.5 22.0 %collective-permute-start.8 = (bf16[512,256]{1,0:T(8,128)(2,1)S(1)}, bf16[512,256]{1,0:T(8,128)(2,1)S(1)}, u32[]{:S(2)}, u32[]{:S(2)}) collective-permute-start(bf16[512,256]{1,0:T(8,128)(2,1)S(1)} %get-tuple-element.110), channel_id=1, source_target_pairs={{0,3},{1,2},{2,1},{3,0},{4,7},{5,6},{6,5},{7,4},{8,11},{9,10},{10,... | collective-permute-start | bytes 786440 | tf_op jit(solution)/shard_map/ppermute | solution.py:524
  49.7 22.3 %collective-permute-start.10 = (bf16[512,256]{1,0:T(8,128)(2,1)S(1)}, bf16[512,256]{1,0:T(8,128)(2,1)S(1)}, u32[]{:S(2)}, u32[]{:S(2)}) collective-permute-start(bf16[512,256]{1,0:T(8,128)(2,1)S(1)} %get-tuple-element.112), channel_id=1, source_target_pairs={{0,3},{1,2},{2,1},{3,0},{4,7},{5,6},{6,5},{7,4},{8,11},{9,10},{10,... | collective-permute-start | bytes 786440 | tf_op jit(solution)/shard_map/ppermute | solution.py:524
  51.5 24.6 %collective-permute-start.16 = (bf16[512,256]{1,0:T(8,128)(2,1)S(1)}, bf16[512,256]{1,0:T(8,128)(2,1)S(1)}, u32[]{:S(2)}, u32[]{:S(2)}) collective-permute-start(bf16[512,256]{1,0:T(8,128)(2,1)S(1)} %get-tuple-element.122), channel_id=1, source_target_pairs={{0,1},{1,0},{2,3},{3,2},{4,5},{5,4},{6,7},{7,6},{8,9},{9,8},{10,11... | collective-permute-start | bytes 786440 | tf_op jit(solution)/shard_map/ppermute | solution.py:524
  55.6 20.6 %collective-permute-start.23 = (bf16[512,256]{1,0:T(8,128)(2,1)S(1)}, bf16[512,256]{1,0:T(8,128)(2,1)S(1)}, u32[]{:S(2)}, u32[]{:S(2)}) collective-permute-start(bf16[512,256]{1,0:T(8,128)(2,1)S(1)} %get-tuple-element.129), channel_id=1, source_target_pairs={{0,1},{1,0},{2,3},{3,2},{4,5},{5,4},{6,7},{7,6},{8,9},{9,8},{10,11... | collective-permute-start | bytes 786440 | tf_op jit(solution)/shard_map/ppermute | solution.py:524
  60.8 19.7 %collective-permute-start.20 = (bf16[512,256]{1,0:T(8,128)(2,1)S(1)}, bf16[512,256]{1,0:T(8,128)(2,1)S(1)}, u32[]{:S(2)}, u32[]{:S(2)}) collective-permute-start(bf16[512,256]{1,0:T(8,128)(2,1)S(1)} %get-tuple-element.126), channel_id=1, source_target_pairs={{0,1},{1,0},{2,3},{3,2},{4,5},{5,4},{6,7},{7,6},{8,9},{9,8},{10,11... | collective-permute-start | bytes 786440 | tf_op jit(solution)/shard_map/ppermute | solution.py:524
  82.5 18.4 %collective-permute-start.14 = (bf16[512,256]{1,0:T(8,128)(2,1)S(1)}, bf16[512,256]{1,0:T(8,128)(2,1)S(1)}, u32[]{:S(2)}, u32[]{:S(2)}) collective-permute-start(bf16[512,256]{1,0:T(8,128)(2,1)S(1)} %get-tuple-element.120), channel_id=1, source_target_pairs={{0,2},{1,3},{2,0},{3,1},{4,6},{5,7},{6,4},{7,5},{8,10},{9,11},{10,... | collective-permute-start | bytes 786440 | tf_op jit(solution)/shard_map/ppermute | solution.py:524
  83.3 22.5 %collective-permute-start.15 = (bf16[512,256]{1,0:T(8,128)(2,1)S(1)}, bf16[512,256]{1,0:T(8,128)(2,1)S(1)}, u32[]{:S(2)}, u32[]{:S(2)}) collective-permute-start(bf16[512,256]{1,0:T(8,128)(2,1)S(1)} %get-tuple-element.121), channel_id=1, source_target_pairs={{0,3},{1,2},{2,1},{3,0},{4,7},{5,6},{6,5},{7,4},{8,11},{9,10},{10,... | collective-permute-start | bytes 786440 | tf_op jit(solution)/shard_map/ppermute | solution.py:524
  108.0 20.3 %collective-permute-start.32 = (bf16[512,256]{1,0:T(8,128)(2,1)}, bf16[512,256]{1,0:T(8,128)(2,1)}, u32[]{:S(2)}, u32[]{:S(2)}) collective-permute-start(bf16[512,256]{1,0:T(8,128)(2,1)} %get-tuple-element.157), channel_id=1, source_target_pairs={{0,3},{1,2},{2,1},{3,0},{4,7},{5,6},{6,5},{7,4},{8,11},{9,10},{10,... | collective-permute-start | bytes 786440 | tf_op jit(solution)/shard_map/ppermute | solution.py:524
  115.8 93.4 %all-reduce.2.cloned.1.call-start = ((), (), s32[]{:S(2)}) async-start(), calls=%async_computation | async-start | bytes 2097152 | tf_op jit(solution)/shard_map/psum | solution.py:645
  115.8 29.2 %collective-permute-start.27 = (bf16[512,256]{1,0:T(8,128)(2,1)}, bf16[512,256]{1,0:T(8,128)(2,1)}, u32[]{:S(2)}, u32[]{:S(2)}) collective-permute-start(bf16[512,256]{1,0:T(8,128)(2,1)} %copy-done.26), channel_id=1, source_target_pairs={{0,1},{1,0},{2,3},{3,2},{4,5},{5,4},{6,7},{7,6},{8,9},{9,8},{10,11... | collective-permute-start | bytes 786440 | tf_op jit(solution)/shard_map/ppermute | solution.py:524
  117.1 27.9 %collective-permute-start.28 = (bf16[512,256]{1,0:T(8,128)(2,1)S(1)}, bf16[512,256]{1,0:T(8,128)(2,1)}, u32[]{:S(2)}, u32[]{:S(2)}) collective-permute-start(bf16[512,256]{1,0:T(8,128)(2,1)S(1)} %get-tuple-element.153), channel_id=1, source_target_pairs={{0,2},{1,3},{2,0},{3,1},{4,6},{5,7},{6,4},{7,5},{8,10},{9,11},{10,... | collective-permute-start | bytes 786440 | tf_op jit(solution)/shard_map/ppermute | solution.py:524
  118.0 27.0 %collective-permute-start.29 = (bf16[512,256]{1,0:T(8,128)(2,1)S(1)}, bf16[512,256]{1,0:T(8,128)(2,1)}, u32[]{:S(2)}, u32[]{:S(2)}) collective-permute-start(bf16[512,256]{1,0:T(8,128)(2,1)S(1)} %get-tuple-element.154), channel_id=1, source_target_pairs={{0,3},{1,2},{2,1},{3,0},{4,7},{5,6},{6,5},{7,4},{8,11},{9,10},{10,... | collective-permute-start | bytes 786440 | tf_op jit(solution)/shard_map/ppermute | solution.py:524
  123.1 24.9 %collective-permute-start.25 = (bf16[512,256]{1,0:T(8,128)(2,1)}, bf16[512,256]{1,0:T(8,128)(2,1)S(1)}, u32[]{:S(2)}, u32[]{:S(2)}) collective-permute-start(bf16[512,256]{1,0:T(8,128)(2,1)} %get-tuple-element.150), channel_id=1, source_target_pairs={{0,2},{1,3},{2,0},{3,1},{4,6},{5,7},{6,4},{7,5},{8,10},{9,11},{10,... | collective-permute-start | bytes 786440 | tf_op jit(solution)/shard_map/ppermute | solution.py:524
  128.3 21.2 %collective-permute-start.26 = (bf16[512,256]{1,0:T(8,128)(2,1)S(1)}, bf16[512,256]{1,0:T(8,128)(2,1)S(1)}, u32[]{:S(2)}, u32[]{:S(2)}) collective-permute-start(bf16[512,256]{1,0:T(8,128)(2,1)S(1)} %get-tuple-element.151), channel_id=1, source_target_pairs={{0,3},{1,2},{2,1},{3,0},{4,7},{5,6},{6,5},{7,4},{8,11},{9,10},{10,... | collective-permute-start | bytes 786440 | tf_op jit(solution)/shard_map/ppermute | solution.py:524
  150.2 35.1 %collective-permute-start.40 = (bf16[512,768]{1,0:T(8,128)(2,1)}, bf16[512,768]{1,0:T(8,128)(2,1)S(1)}, u32[]{:S(2)}, u32[]{:S(2)}) collective-permute-start(bf16[512,768]{1,0:T(8,128)(2,1)} %get-tuple-element.172), channel_id=1, source_target_pairs={{0,1},{1,0},{2,3},{3,2},{4,5},{5,4},{6,7},{7,6},{8,9},{9,8},{10,11... | collective-permute-start | bytes 2359304 | tf_op jit(solution)/shard_map/ppermute | solution.py:524
  151.2 35.8 %collective-permute-start.41 = (bf16[512,768]{1,0:T(8,128)(2,1)}, bf16[512,768]{1,0:T(8,128)(2,1)S(1)}, u32[]{:S(2)}, u32[]{:S(2)}) collective-permute-start(bf16[512,768]{1,0:T(8,128)(2,1)} %get-tuple-element.173), channel_id=1, source_target_pairs={{0,2},{1,3},{2,0},{3,1},{4,6},{5,7},{6,4},{7,5},{8,10},{9,11},{10,... | collective-permute-start | bytes 2359304 | tf_op jit(solution)/shard_map/ppermute | solution.py:524
  152.9 36.2 %collective-permute-start.42 = (bf16[512,768]{1,0:T(8,128)(2,1)}, bf16[512,768]{1,0:T(8,128)(2,1)}, u32[]{:S(2)}, u32[]{:S(2)}) collective-permute-start(bf16[512,768]{1,0:T(8,128)(2,1)} %get-tuple-element.174), channel_id=1, source_target_pairs={{0,3},{1,2},{2,1},{3,0},{4,7},{5,6},{6,5},{7,4},{8,11},{9,10},{10,... | collective-permute-start | bytes 2359304 | tf_op jit(solution)/shard_map/ppermute | solution.py:524
  185.4 30.7 %collective-permute-start.37 = (bf16[512,256]{1,0:T(8,128)(2,1)}, bf16[512,256]{1,0:T(8,128)(2,1)S(1)}, u32[]{:S(2)}, u32[]{:S(2)}) collective-permute-start(bf16[512,256]{1,0:T(8,128)(2,1)} %get-tuple-element.169), channel_id=1, source_target_pairs={{0,1},{1,0},{2,3},{3,2},{4,5},{5,4},{6,7},{7,6},{8,9},{9,8},{10,11... | collective-permute-start | bytes 786440 | tf_op jit(solution)/shard_map/ppermute | solution.py:524
  185.4 30.7 %collective-permute-start.38 = (bf16[512,256]{1,0:T(8,128)(2,1)}, bf16[512,256]{1,0:T(8,128)(2,1)S(1)}, u32[]{:S(2)}, u32[]{:S(2)}) collective-permute-start(bf16[512,256]{1,0:T(8,128)(2,1)} %get-tuple-element.170), channel_id=1, source_target_pairs={{0,2},{1,3},{2,0},{3,1},{4,6},{5,7},{6,4},{7,5},{8,10},{9,11},{10,... | collective-permute-start | bytes 786440 | tf_op jit(solution)/shard_map/ppermute | solution.py:524
  187.0 27.7 %collective-permute-start.47 = (bf16[256,128]{1,0:T(8,128)(2,1)S(1)}, bf16[256,128]{1,0:T(8,128)(2,1)S(1)}, u32[]{:S(2)}, u32[]{:S(2)}) collective-permute-start(bf16[256,128]{1,0:T(8,128)(2,1)S(1)} %add_up.1.refs_12_.refs_1_), channel_id=1, source_target_pairs={{0,16},{4,20},{8,24},{12,28},{16,0},{20,4},{24,8},{28,12},{1,17},{... | collective-permute-start | bytes 196616 | tf_op jit(solution)/shard_map/ppermute | solution.py:524
  189.1 25.6 %collective-permute-start.48 = (bf16[256,128]{1,0:T(8,128)(2,1)S(1)}, bf16[256,128]{1,0:T(8,128)(2,1)S(1)}, u32[]{:S(2)}, u32[]{:S(2)}) collective-permute-start(bf16[256,128]{1,0:T(8,128)(2,1)S(1)} %add_up.1.refs_12_.refs_1_), channel_id=1, source_target_pairs={{0,24},{4,28},{8,16},{12,20},{16,8},{20,12},{24,0},{28,4},{1,25},{... | collective-permute-start | bytes 196616 | tf_op jit(solution)/shard_map/ppermute | solution.py:524
  (63 other events, 555.1 us)
Sparse Core Ops, SparseCore 0:
  130.4 78.7 all-reduce.1
